TPU v7x, 512 devices: a whole 4x4x16 slice. The times are simulated.
512 devices in a mesh: roll: 64 (over z, x_lo, core), head: 8 (over x_hi, y).
Axes of the slice: x: 4 (x_hi: 2, x_lo: 2; x = x_hi * 2 + x_lo), y: 4, z: 16, core: 2. Of those that a mesh axis runs over, the one named last changes fastest.
Arguments:
- query: bfloat16 [64, 128, 8192], P('roll', None, 'head'), may hold values from -48 to 48
- resp_kv: bfloat16 [64, 128, 2048], P('roll', None, 'head'), may hold values from -6 to 6
- grad_out: bfloat16 [64, 128, 8192], P('roll', None, 'head'), may hold values from -6 to 6
- prefix_kv: bfloat16 [4096, 2048], P('roll', 'head'), may hold values from -6 to 6
- lengths: int32 [64], replicated, may hold values from 1 to 128, 5120 in all
- order: int32 [64], P('roll'), may hold values from 0 to 63, each once
Outputs:
- d_query: bfloat16 [64, 128, 8192], P('roll', None, 'head')
- d_resp_kv: bfloat16 [64, 128, 2048], P('roll', 'head')
- d_prefix: float32 [4096, 2048], P('roll', 'head')
Inputs may be any that keep to these rules, and one draw needn't show every extreme that they name: order holds each response number once.
All inputs are finite; a program needn't handle non-finite values.
Results may differ from a plain program's by a relative error of at most 0.012.
The roundings to bfloat16 on the way count: a program that leaves them out, or rounds other values in their place, can miss the bound.
Values may be sent and summed in bfloat16 or wider, within the bound.
No kernel may reach another device: no remote copies, remote signals or barrier semaphores. Data moves between devices by JAX's collectives and lax.ppermute only.
A program may use at most 64 MiB of HBM per device.

v0:
```python
import math

import jax
import jax.numpy as jnp
from jax import lax
from jax.sharding import PartitionSpec as P


def one_head(inputs, response_keys, response_values, prompt_keys, prompt_values, live):
    query_matrix, gradient_list = inputs
    length = query_matrix.shape[0]
    width = query_matrix.shape[1]
    score_scale = 1.0 / math.sqrt(width)
    prompt_scores = (
        jnp.dot(query_matrix, prompt_keys.T, preferred_element_type=jnp.float32) * score_scale
    )
    response_scores = (
        jnp.dot(query_matrix, response_keys.T, preferred_element_type=jnp.float32) * score_scale
    )
    position = jnp.arange(length)
    response_scores = jnp.where(position[:, None] >= position[None, :], response_scores, -jnp.inf)
    top = jnp.maximum(jnp.max(prompt_scores, -1), jnp.max(response_scores, -1))
    prompt_exp = jnp.exp(prompt_scores - top[:, None])
    own_exp = jnp.exp(response_scores - top[:, None])
    total = jnp.sum(prompt_exp, -1) + jnp.sum(own_exp, -1)
    valid = (position < live).astype(jnp.float32)
    factor = valid / total
    prompt_w = prompt_exp * factor[:, None]
    own_w = own_exp * factor[:, None]
    prompt_weight_bwd = prompt_w.astype(jnp.bfloat16)
    response_weight_bwd = own_w.astype(jnp.bfloat16)
    attended_output = jnp.dot(prompt_weight_bwd, prompt_values, preferred_element_type=jnp.float32)
    attended_output = attended_output + jnp.dot(
        response_weight_bwd, response_values, preferred_element_type=jnp.float32
    )
    delta = jnp.sum(gradient_list.astype(jnp.float32) * attended_output, -1)
    prompt_dp = jnp.dot(gradient_list, prompt_values.T, preferred_element_type=jnp.float32)
    response_weight_gradient = jnp.dot(
        gradient_list, response_values.T, preferred_element_type=jnp.float32
    )
    prompt_score_gradient = (prompt_w * (prompt_dp - delta[:, None]) * score_scale).astype(
        jnp.bfloat16
    )
    response_score_gradient = (
        own_w * (response_weight_gradient - delta[:, None]) * score_scale
    ).astype(jnp.bfloat16)
    query_gradient = jnp.dot(prompt_score_gradient, prompt_keys, preferred_element_type=jnp.float32)
    query_gradient = query_gradient + jnp.dot(
        response_score_gradient, response_keys, preferred_element_type=jnp.float32
    )
    response_key_gradient = jnp.dot(
        response_score_gradient.T, query_matrix, preferred_element_type=jnp.float32
    )
    response_value_gradient = jnp.dot(
        response_weight_bwd.T, gradient_list, preferred_element_type=jnp.float32
    )
    return (
        query_gradient,
        response_key_gradient,
        response_value_gradient,
        prompt_score_gradient,
        prompt_weight_bwd,
    )


def one_response(inputs, prompt_keys, prompt_values, width):
    query_rows, kv_rows, grad_rows, live = inputs
    length = query_rows.shape[0]
    group = query_rows.shape[1] // width
    query_matrix = jnp.transpose(query_rows.reshape(length, group, width), (1, 0, 2))
    gradient_list = jnp.transpose(grad_rows.reshape(length, group, width), (1, 0, 2))
    response_keys = kv_rows[:, :width]
    response_values = kv_rows[:, width:]
    (
        query_gradient,
        response_key_gradient,
        response_value_gradient,
        prompt_score_gradient,
        prompt_weight_bwd,
    ) = lax.map(
        lambda pair: one_head(
            pair, response_keys, response_values, prompt_keys, prompt_values, live
        ),
        (query_matrix, gradient_list),
    )
    d_rows = (
        jnp.transpose(query_gradient, (1, 0, 2)).reshape(length, group * width).astype(jnp.bfloat16)
    )
    d_own = jnp.concatenate(
        [jnp.sum(response_key_gradient, 0), jnp.sum(response_value_gradient, 0)], 1
    ).astype(jnp.bfloat16)
    return (d_rows, d_own, prompt_score_gradient, prompt_weight_bwd)


def per_device(query, resp_kv, grad_out, prefix_kv, lengths, order):
    width = resp_kv.shape[2] // 2
    responses = query.shape[0]
    length = query.shape[1]
    group = query.shape[2] // width
    count = lengths.shape[0]
    picked = order[:, None] == jnp.arange(count, dtype=jnp.int32)[None, :]
    live = jnp.sum(jnp.where(picked, lengths[None, :], 0), axis=1)
    prompt = lax.all_gather(prefix_kv, "roll", axis=0, tiled=True)
    prompt_keys = prompt[:, :width]
    prompt_values = prompt[:, width:]
    d_query, d_own, scores_grad, weights = lax.map(
        lambda inputs: one_response(inputs, prompt_keys, prompt_values, width),
        (query, resp_kv, grad_out, live),
    )
    query_matrix = query.reshape(responses, length, group, width)
    gradient_list = grad_out.reshape(responses, length, group, width)
    keys_term = jnp.einsum(
        "rglp,rlgd->pd", scores_grad, query_matrix, preferred_element_type=jnp.float32
    )
    values_term = jnp.einsum(
        "rglp,rlgd->pd", weights, gradient_list, preferred_element_type=jnp.float32
    )
    d_prefix = lax.psum_scatter(
        jnp.concatenate([keys_term, values_term], 1), "roll", scatter_dimension=0, tiled=True
    )
    d_own_split = lax.all_to_all(d_own, "head", split_axis=1, concat_axis=2, tiled=True)
    return (d_query, d_own_split, d_prefix)


def solution(mesh):
    return jax.shard_map(
        per_device,
        mesh=mesh,
        in_specs=(
            P("roll", None, "head"),
            P("roll", None, "head"),
            P("roll", None, "head"),
            P("roll", "head"),
            P(),
            P("roll"),
        ),
        out_specs=(P("roll", None, "head"), P("roll", "head", None), P("roll", "head")),
        check_vma=False,
    )
```

profile of v0, /device:TPU:24, one launch (start us, length us, event | category | flops | bytes accessed | tf_op | source)
XLA Modules:
  0.0 450.2 jit_solution(1556752678655909395)
XLA Ops:
  8.0 1.1 copy.36
  9.1 1.1 copy.35
  10.9 1.3 fusion.34
  13.0 123.5 %all-gather.2.cloned.1.call-done = bf16[4096,256]{1,0:T(8,128)(2,1)} async-done(((bf16[64,256]{1,0:T(8,128)(2,1)}), bf16[4096,256]{1,0:T(8,128)(2,1)}) %all-gather.2.cloned.1.call-update) | async-done | bytes 2097168 | tf_op jit(solution)/shard_map/all_gather | solution.py:103
  136.5 1.7 fusion.37
  138.2 61.2 %while.32 = (s32[]{:T(128)}, bf16[8,128,128]{2,1,0:T(8,128)(2,1)S(1)}, f32[8,128,128]{2,1,0:T(8,128)S(1)}, f32[8,128,128]{2,1,0:T(8,128)}, bf16[8,128,4096]{2,1,...) while((s32[]{:T(128)}, ...), condition=%wide.region_7.8_spmd, body=%wide.region_1.7_spmd.sunk | while | flops 569229312 | bytes 20136092 | solution.py:80
  140.1 1.5 bitcast_dynamic-update-slice_fusion.4
  142.3 1.8 bitcast_dynamic-update-slice_fusion.5
  147.8 1.4 bitcast_dynamic-update-slice_fusion.4
  149.9 1.9 bitcast_dynamic-update-slice_fusion.5
  155.4 1.4 bitcast_dynamic-update-slice_fusion.4
  157.6 1.8 bitcast_dynamic-update-slice_fusion.5
  163.0 1.4 bitcast_dynamic-update-slice_fusion.4
  165.2 1.8 bitcast_dynamic-update-slice_fusion.5
  170.6 1.4 bitcast_dynamic-update-slice_fusion.4
  172.9 1.8 bitcast_dynamic-update-slice_fusion.5
  178.3 1.4 bitcast_dynamic-update-slice_fusion.4
  180.5 1.9 bitcast_dynamic-update-slice_fusion.5
  186.0 1.4 bitcast_dynamic-update-slice_fusion.4
  188.1 1.9 bitcast_dynamic-update-slice_fusion.5
  193.6 1.4 bitcast_dynamic-update-slice_fusion.4
  195.8 1.8 bitcast_dynamic-update-slice_fusion.5
  199.3 4.8 %convolution_bitcast_fusion.2 = f32[4096,128]{0,1:T(8,128)S(1)} fusion(bf16[128,8,128]{0,2,1:T(8,128)(2,1)S(1)} %bitcast.137, bf16[8,128,4096]{2,1,0:T(8,128)(2,1)} %get-tuple-element.111), kind=kOutput, calls=%fused_computation.50 | convolution fusion | flops 1073741824 | bytes 10747904 | tf_op jit(solution)/shard_map/rglp,rlgd->pd/dot_general | solution.py:115
  204.1 1.0 copy-done
  205.1 1.4 convolution_bitcast_fusion.3
  206.5 2.4 pad_maximum_fusion
  208.9 5.6 %copy.43 = f32[4096,256]{1,0:T(8,128)} copy(f32[4096,256]{0,1:T(8,128)} %pad_maximum_fusion) | data formatting | bytes 8388608
  214.5 1.1 reduce_sum.58
  216.3 1.0 reduce.2
  218.0 6.9 %all-to-all-start = ((bf16[8,2,2048]{2,1,0:T(2,128)(2,1)}), bf16[8,2,2048]{2,1,0:T(2,128)(2,1)S(1)}, u32[]{:S(2)}, u32[]{:S(2)}) async-start(bf16[8,2,2048]{2,1,0:T(2,128)(2,1)} %reshape.101), calls=%async_computation | async-start | bytes 131072 | tf_op jit(solution)/shard_map/all_to_all | solution.py:121
  225.9 4.8 %all-to-all-done = bf16[8,2,2048]{2,1,0:T(2,128)(2,1)S(1)} async-done(((bf16[8,2,2048]{2,1,0:T(2,128)(2,1)}), bf16[8,2,2048]{2,1,0:T(2,128)(2,1)S(1)}, u32[]{:S(2)}, u32[]{:S(2)}) %all-to-all-start) | async-done | bytes 65568 | tf_op jit(solution)/shard_map/all_to_all | solution.py:121
  231.4 211.9 %reduce-scatter.4.cloned.1.call-done = f32[64,256]{1,0:T(8,128)} async-done(((f32[4096,256]{1,0:T(8,128)}), f32[64,256]{1,0:T(8,128)}) %reduce-scatter.4.cloned.1.call-update) | async-done | bytes 65552
  (125 shorter events, 39.5 us)
Async XLA Ops:
  7.2 129.3 %all-gather.2.cloned.1.call-start = ((), (), s32[]{:S(2)}) async-start(), calls=%async_computation.2 | async-start | bytes 2129920 | tf_op jit(solution)/shard_map/all_gather | solution.py:103
  7.9 435.4 %reduce-scatter.4.cloned.1.call-start = ((), (), s32[]{:S(2)}) async-start(), calls=%async_computation.3 | async-start | bytes 4259840
  199.3 5.8 %copy-start = (bf16[8,128,4096]{2,1,0:T(8,128)(2,1)S(1)}, bf16[8,128,4096]{2,1,0:T(8,128)(2,1)}, u32[]{:S(2)}) copy-start(bf16[8,128,4096]{2,1,0:T(8,128)(2,1)} %get-tuple-element.110) | copy-start | bytes 25165828
  218.0 12.7 %all-to-all-start = ((bf16[8,2,2048]{2,1,0:T(2,128)(2,1)}), bf16[8,2,2048]{2,1,0:T(2,128)(2,1)S(1)}, u32[]{:S(2)}, u32[]{:S(2)}) async-start(bf16[8,2,2048]{2,1,0:T(2,128)(2,1)} %reshape.101), calls=%async_computation | async-start | bytes 131072 | tf_op jit(solution)/shard_map/all_to_all | solution.py:121
Sparse Core Ops, SparseCore 0:
  10.1 126.2 all-gather.1
  214.7 228.6 reduce-scatter.3
where the time goes:
time: 451 us; the launch traced here: 450 us
  waiting for transfers between devices  341 us (76%)
  matrix products  46.7 us (10%)
  other arithmetic  26.2 us (6%)
  between operations  14.8 us (3%)
  local copies, waits for them, and re-layouts  14.2 us (3%)
  starting transfers between devices  7.01 us (2%)
    unnamed x3, waiting for transfers between devices  213 us
    all_gather x1, waiting for transfers between devices, per_device(): prompt = lax.all_gather(prefix_kv, 'roll', axis=0, tiled=True)  124 us
    dot_general x8, matrix products, one_head(): jnp.dot(gradient_list, prompt_values.T, preferred_element_type=jnp.float32)  14.8 us
    dynamic_update_slice x8, other arithmetic, one_response(): lax.map(lambda pair: one_head(pair, response_keys, response_values, promp...  11.1 us
    unnamed x9, local copies, waits for them, and re-layouts  10 us
  transfers between devices with their start and end apart: 3, of which 3 were waited for; matrix products, arithmetic and copies ran while one was open for 2% of the time, Pallas kernels for 0%

commit v1 on v0

v1 whole, which is shorter than its diff:
```python
import functools
import math

import jax
import jax.numpy as jnp
from jax import lax
from jax.experimental import pallas as pl
from jax.experimental.pallas import tpu as pltpu
from jax.sharding import PartitionSpec as P

F32 = jnp.float32
BF16 = jnp.bfloat16
NEG = -1e30
CHUNK = 256
VMEM_LIMIT = 56 * 1024 * 1024


def nt(a, b):
    return lax.dot_general(a, b, (((1,), (1,)), ((), ())), preferred_element_type=F32)


def nn(a, b):
    return lax.dot_general(a, b, (((1,), (0,)), ((), ())), preferred_element_type=F32)


def tn(a, b):
    return lax.dot_general(a, b, (((0,), (0,)), ((), ())), preferred_element_type=F32)


def stack_heads(src, dst, width, group):
    length = src.shape[0]
    for h in range(group):
        dst[h * length:(h + 1) * length, :] = src[:, h * width:(h + 1) * width]


def forward_kernel(
    lengths, order, q_ref, g_ref, own_ref, *rest, width, group, blocks
):
    kv = rest[:blocks]
    dv = rest[blocks:2 * blocks]
    stats_ref, d_own_ref, dq_ref, s_ref, qr, gr = rest[2 * blocks:]
    length = q_ref.shape[0]
    rows = group * length
    per_block = kv[0].shape[0]
    steps = per_block // CHUNK
    scale = 1.0 / math.sqrt(width)
    rate = scale * math.log2(math.e)
    stack_heads(q_ref, qr, width, group)
    stack_heads(g_ref, gr, width, group)

    def fold(s, m, l):
        s3 = s.reshape(s.shape[0] // 8, 8, rows)
        m_new = jnp.maximum(m, jnp.max(s3, axis=0))
        p = jnp.exp2((s3 - m_new[None]) * rate)
        return m_new, l * jnp.exp2((m - m_new) * rate) + jnp.sum(p, axis=0)

    m = jnp.full((8, rows), NEG, F32)
    l = jnp.zeros((8, rows), F32)
    for b in range(blocks):
        def score(i, carry, b=b):
            keys = kv[b][pl.ds(i * CHUNK, CHUNK), :width]
            s = nt(keys, qr[...])
            s_ref[pl.ds(b * per_block + i * CHUNK, CHUNK), :] = s
            return fold(s, *carry)
        m, l = lax.fori_loop(0, steps, score, (m, l))

    own_k = own_ref[:, :width]
    own_v = own_ref[:, width:]
    slot = lax.rem(lax.broadcasted_iota(jnp.int32, (length, rows), 1), length)
    seen = lax.broadcasted_iota(jnp.int32, (length, rows), 0) <= slot
    s_own = jnp.where(seen, nt(own_k, qr[...]), NEG)
    m, l = fold(s_own, m, l)
    top = jnp.max(m, axis=0, keepdims=True)
    total = jnp.sum(l * jnp.exp2((m - top) * rate), axis=0, keepdims=True)
    live = lengths[order[0]]
    factor = jnp.where(slot[:1] < live, 1.0 / total, 0.0)

    out = jnp.zeros((width, rows), F32)
    for b in range(blocks):
        def values(i, out, b=b):
            at = pl.ds(i * CHUNK, CHUNK)
            s = s_ref[pl.ds(b * per_block + i * CHUNK, CHUNK), :]
            w = (jnp.exp2((s - top) * rate) * factor).astype(BF16)
            dv[b][at, :] = nn(w, gr[...]).astype(dv[b].dtype)
            return out + tn(kv[b][at, width:], w)
        out = lax.fori_loop(0, steps, values, out)

    w_own = jnp.exp2((s_own - top) * rate) * factor
    w_own16 = w_own.astype(BF16)
    out = out + tn(own_v, w_own16)
    delta = jnp.sum(gr[...].T.astype(F32) * out, axis=0, keepdims=True)
    dp = nt(own_v, gr[...])
    ds = (w_own * (dp - delta) * scale).astype(BF16)
    d_own_ref[:, :width] = nn(ds, qr[...]).astype(BF16)
    d_own_ref[:, width:] = nn(w_own16, gr[...]).astype(BF16)
    dq_ref[...] = tn(own_k, ds)
    stats_ref[0:1, :] = top
    stats_ref[1:2, :] = factor * scale
    stats_ref[2:3, :] = delta
    stats_ref[3:8, :] = jnp.zeros((5, rows), F32)


def backward_kernel(q_ref, g_ref, stats_ref, dq_in, *rest, width, group, blocks, last):
    kv = rest[:blocks]
    dk = rest[blocks:2 * blocks]
    dq_out, qr, gr = rest[2 * blocks:]
    length = q_ref.shape[0]
    steps = kv[0].shape[0] // CHUNK
    rate = math.log2(math.e) / math.sqrt(width)
    stack_heads(q_ref, qr, width, group)
    stack_heads(g_ref, gr, width, group)
    top = stats_ref[0:1, :]
    factor = stats_ref[1:2, :]
    delta = stats_ref[2:3, :]
    dq = dq_in[...]
    for b in range(blocks):
        def step(i, dq, b=b):
            at = pl.ds(i * CHUNK, CHUNK)
            keys = kv[b][at, :width]
            s = nt(keys, qr[...])
            dp = nt(kv[b][at, width:], gr[...])
            ds = (jnp.exp2((s - top) * rate) * factor * (dp - delta)).astype(BF16)
            dk[b][at, :] = nn(ds, qr[...]).astype(dk[b].dtype)
            return dq + tn(keys, ds)
        dq = lax.fori_loop(0, steps, step, dq)
    if last:
        for h in range(group):
            part = dq[:, h * length:(h + 1) * length]
            dq_out[:, h * width:(h + 1) * width] = part.T.astype(BF16)
    else:
        dq_out[...] = dq


VM = pl.BlockSpec(memory_space=pltpu.VMEM)
SM = pl.BlockSpec(memory_space=pltpu.SMEM)


def run_forward(lengths, order, q, g, own, kv, dv_types, width):
    length = q.shape[0]
    group = q.shape[1] // width
    rows = group * length
    per_block = kv[0].shape[0]
    prompt = per_block * len(kv)
    return pl.pallas_call(
        functools.partial(forward_kernel, width=width, group=group, blocks=len(kv)),
        out_shape=[jax.ShapeDtypeStruct((per_block, width), t) for t in dv_types]
        + [
            jax.ShapeDtypeStruct((8, rows), F32),
            jax.ShapeDtypeStruct((length, 2 * width), BF16),
            jax.ShapeDtypeStruct((width, rows), F32),
        ],
        in_specs=[SM, SM] + [VM] * (3 + len(kv)),
        out_specs=[VM] * (len(kv) + 3),
        scratch_shapes=[
            pltpu.VMEM((prompt, rows), F32),
            pltpu.VMEM((rows, width), BF16),
            pltpu.VMEM((rows, width), BF16),
        ],
        compiler_params=pltpu.CompilerParams(vmem_limit_bytes=VMEM_LIMIT),
        cost_estimate=pl.CostEstimate(
            flops=10 * prompt * rows * width, bytes_accessed=1 << 22, transcendentals=0
        ),
        name="forward",
    )(lengths, order, q, g, own, *kv)


def run_backward(q, g, stats, dq, kv, dk_types, width, last):
    length = q.shape[0]
    group = q.shape[1] // width
    rows = group * length
    per_block = kv[0].shape[0]
    prompt = per_block * len(kv)
    dq_type = (
        jax.ShapeDtypeStruct((length, group * width), BF16)
        if last
        else jax.ShapeDtypeStruct((width, rows), F32)
    )
    return pl.pallas_call(
        functools.partial(
            backward_kernel, width=width, group=group, blocks=len(kv), last=last
        ),
        out_shape=[jax.ShapeDtypeStruct((per_block, width), t) for t in dk_types] + [dq_type],
        in_specs=[VM] * (4 + len(kv)),
        out_specs=[VM] * (len(kv) + 1),
        scratch_shapes=[
            pltpu.VMEM((rows, width), BF16),
            pltpu.VMEM((rows, width), BF16),
        ],
        compiler_params=pltpu.CompilerParams(vmem_limit_bytes=VMEM_LIMIT),
        cost_estimate=pl.CostEstimate(
            flops=14 * prompt * rows * width, bytes_accessed=1 << 22, transcendentals=0
        ),
        name="backward",
    )(q, g, stats, dq, *kv)


def per_device(query, resp_kv, grad_out, prefix_kv, lengths, order, *, layers):
    width = resp_kv.shape[2] // 2
    shard = prefix_kv.shape[0]
    q, g, own = query[0], grad_out[0], resp_kv[0]
    to_core = [(i, i ^ 1) for i in range(4 * layers)]
    to_x = [(i, i ^ 2) for i in range(4 * layers)]
    rings = [[4 * z + i for z in range(layers)] for i in range(4)]

    kv_mine = lax.all_gather(prefix_kv, "roll", axis=0, tiled=True, axis_index_groups=rings)
    kv_x = lax.ppermute(kv_mine, "roll", to_x)
    kv_core = lax.ppermute(kv_mine, "roll", to_core)
    kv_diag = lax.ppermute(kv_x, "roll", to_core)

    dv_core, dv_diag, dv_x, dv_mine, stats, d_own, dq = run_forward(
        lengths, order, q, g, own, [kv_core, kv_diag, kv_x, kv_mine],
        [BF16, BF16, F32, F32], width,
    )
    parts = d_own.reshape(8, d_own.shape[0] // 8, 2 * width)
    parts = lax.all_to_all(parts, "head", split_axis=0, concat_axis=0, tiled=True)
    d_resp = jnp.transpose(parts, (1, 0, 2)).reshape(1, parts.shape[1], -1)

    dk_core, dk_diag, dq = run_backward(
        q, g, stats, dq, [kv_core, kv_diag], [BF16, BF16], width, False
    )
    dk_x, dk_mine, d_query = run_backward(
        q, g, stats, dq, [kv_x, kv_mine], [F32, F32], width, True
    )

    def collect(core, diag, x, mine):
        got_mine = lax.ppermute(core, "roll", to_core)
        got_x = lax.ppermute(diag, "roll", to_core)
        over = lax.ppermute((x + got_x).astype(BF16), "roll", to_x)
        term = (mine + got_mine + over).astype(BF16).reshape(layers, shard, width)
        terms = lax.all_to_all(
            term, "roll", split_axis=0, concat_axis=0, tiled=True, axis_index_groups=rings
        )
        return jnp.sum(terms.astype(F32), axis=0)

    values = collect(dv_core, dv_diag, dv_x, dv_mine)
    keys = collect(dk_core, dk_diag, dk_x, dk_mine)
    return d_query[None], d_resp, jnp.concatenate([keys, values], axis=1)


def solution(mesh):
    layers = mesh.shape["roll"] // 4
    return jax.shard_map(
        functools.partial(per_device, layers=layers),
        mesh=mesh,
        in_specs=(
            P("roll", None, "head"),
            P("roll", None, "head"),
            P("roll", None, "head"),
            P("roll", "head"),
            P(),
            P("roll"),
        ),
        out_specs=(P("roll", None, "head"), P("roll", "head", None), P("roll", "head")),
        check_vma=False,
    )
```

time: 451 us -> 164 us (0.36)
  waiting for transfers between devices: 341 us -> 39.9 us
  matrix products: 46.7 us -> 0 us
  blocking collectives: 0 us -> 38.8 us
  starting transfers between devices: 7.01 us -> 42.6 us
  Pallas kernels: 0 us -> 34.2 us
  other arithmetic: 26.2 us -> 3.52 us
  between operations: 14.8 us -> 1.49 us
  local copies, waits for them, and re-layouts: 14.2 us -> 1.5 us
    unnamed x3 -> x0, waiting for transfers between devices: 213 us -> none
    all_gather x1 -> x0, waiting for transfers between devices: 124 us -> none  [per_device(): prompt = lax.all_gather(prefix_kv, 'roll', axis=0, tiled=True)]
    dot_general x82 -> x0, matrix products: 46.7 us -> none  [the longest x8 14.8 us: one_head(): jnp.dot(gradient_list, prompt_values.T, preferred_element_type=jnp.float32)]
    all_gather x0 -> x1, blocking collectives: none -> 38.8 us  [per_device(): lax.all_gather(prefix_kv, 'roll', axis=0, tiled=True, axis_index_groups=r...]
    pallas_call x0 -> x3, Pallas kernels: none -> 34.2 us  [the longest x1 17.9 us: run_forward(): pl.pallas_call(functools.partial(forward_kernel, width=width, group=group...]
    ppermute x0 -> x9, starting transfers between devices: none -> 21 us  [the longest x2 5.66 us: collect(): over = lax.ppermute((x + got_x).astype(BF16), 'roll', to_x)]
    all_to_all x1 -> x3, waiting for transfers between devices: 4.79 us -> 24.5 us  [the longest x2 21.4 us: collect(): lax.all_to_all(term, 'roll', split_axis=0, concat_axis=0, tiled=True, axi...]
    ppermute x0 -> x9, waiting for transfers between devices: none -> 15.4 us  [the longest x2 8.45 us: collect(): over = lax.ppermute((x + got_x).astype(BF16), 'roll', to_x)]
  transfers between devices with their start and end apart: 3 -> 12, of which waited for: 3 -> 6; matrix products, arithmetic and copies ran while one was open for 2% -> 2% of each run, Pallas kernels for 0% -> 5%
where the time goes in v1:
time: 164 us; the launch traced here: 162 us
  starting transfers between devices  42.6 us (26%)
  waiting for transfers between devices  39.9 us (24%)
  blocking collectives  38.8 us (24%)
  Pallas kernels  34.2 us (21%)
  other arithmetic  3.52 us (2%)
    all_gather x1, blocking collectives, per_device(): lax.all_gather(prefix_kv, 'roll', axis=0, tiled=True, axis_index_groups=r...  38.8 us
    all_to_all x2, waiting for transfers between devices, collect(): lax.all_to_all(term, 'roll', split_axis=0, concat_axis=0, tiled=True, axi...  21.4 us
    pallas_call x1, Pallas kernels, run_forward(): pl.pallas_call(functools.partial(forward_kernel, width=width, group=group...  17.9 us
    pallas_call x2, Pallas kernels, run_backward(): pl.pallas_call(functools.partial(backward_kernel, width=width, group=grou...  16.3 us
    all_to_all x2, starting transfers between devices, collect(): lax.all_to_all(term, 'roll', split_axis=0, concat_axis=0, tiled=True, axi...  14.7 us
    ppermute x2, waiting for transfers between devices, collect(): over = lax.ppermute((x + got_x).astype(BF16), 'roll', to_x)  8.45 us
    all_to_all x1, starting transfers between devices, per_device(): lax.all_to_all(parts, 'head', split_axis=0, concat_axis=0, tiled=True)  6.87 us
    ppermute x1, waiting for transfers between devices, per_device(): kv_x = lax.ppermute(kv_mine, 'roll', to_x)  5.74 us
  transfers between devices with their start and end apart: 12, of which 6 were waited for; matrix products, arithmetic and copies ran while one was open for 2% of the time, Pallas kernels for 5%

profile of v1, /device:TPU:24, one launch (start us, length us, event | category | flops | bytes accessed | tf_op | source)
XLA Modules:
  0.0 162.0 jit_solution(17675929181308925264)
XLA Ops:
  0.6 38.8 %all_gather.3.rest_3_.rest_1_ = bf16[1024,256]{1,0:T(8,128)(2,1)S(1)} all-gather(bf16[64,256]{1,0:T(8,128)(2,1)} %param.9), channel_id=1, replica_groups={{0,32,64,96,128,160,192,224,256,288,320,352,384,416,448,480},{8,40,72,1..., dimensions={0}, use_global_device_ids=true | all-gather | bytes 557056 | tf_op jit(solution)/shard_map/all_gather | solution.py:205
  39.4 3.4 %collective-permute-start.1 = (bf16[1024,256]{1,0:T(8,128)(2,1)S(1)}, bf16[1024,256]{1,0:T(8,128)(2,1)S(1)}, u32[]{:S(2)}, u32[]{:S(2)}) collective-permute-start(bf16[1024,256]{1,0:T(8,128)(2,1)S(1)} %all_gather.3.rest_3_.rest_1_), channel_id=1, source_target_pairs={{0,16},{8,24},{16,0},{24,8},{32,48},{40,56},{48,32},{56,40},{64,80... | collective-permute-start | bytes 1572872 | tf_op jit(solution)/shard_map/ppermute | solution.py:206
  42.8 1.9 %collective-permute-start = (bf16[1024,256]{1,0:T(8,128)(2,1)S(1)}, bf16[1024,256]{1,0:T(8,128)(2,1)S(1)}, u32[]{:S(2)}, u32[]{:S(2)}) collective-permute-start(bf16[1024,256]{1,0:T(8,128)(2,1)S(1)} %all_gather.3.rest_3_.rest_1_), channel_id=1, source_target_pairs={{0,8},{8,0},{16,24},{24,16},{32,40},{40,32},{48,56},{56,48},{64,72... | collective-permute-start | bytes 1572872 | tf_op jit(solution)/shard_map/ppermute | solution.py:207
  44.8 5.7 %collective-permute-done.1.rest_2_.rest_0_ = bf16[1024,256]{1,0:T(8,128)(2,1)S(1)} collective-permute-done((bf16[1024,256]{1,0:T(8,128)(2,1)S(1)}, bf16[1024,256]{1,0:T(8,128)(2,1)S(1)}, u32[]{:S(2)}, u32[]{:S(2)}) %collective-permute-start.1) | collective-permute-done | bytes 524320 | tf_op jit(solution)/shard_map/ppermute | solution.py:206
  50.5 1.9 %collective-permute-start.2 = (bf16[1024,256]{1,0:T(8,128)(2,1)S(1)}, bf16[1024,256]{1,0:T(8,128)(2,1)S(1)}, u32[]{:S(2)}, u32[]{:S(2)}) collective-permute-start(bf16[1024,256]{1,0:T(8,128)(2,1)S(1)} %collective-permute-done.1.rest_2_.rest_0_), channel_id=1, source_target_pairs={{0,8},{8,0},{16,24},{24,16},{32,40},{40,32},{48,56},{56,48},{64,72... | collective-permute-start | bytes 1572872 | tf_op jit(solution)/shard_map/ppermute | solution.py:208
  53.1 0.0 collective-permute-done.rest_0_
  53.1 1.2 collective-permute-done.2.rest_1_
  54.3 0.8 copy-done.6
  55.1 17.9 %forward.1 = (bf16[1024,128]{1,0:T(8,128)(2,1)}, bf16[1024,128]{1,0:T(8,128)(2,1)}, f32[1024,128]{1,0:T(8,128)}, f32[1024,128]{1,0:T(8,128)}, f32[8,1024]{1,0:T(...) custom-call(s32[64]{0:T(128)} %lengths.1, s32[1]{0:T(128)S(6)} %copy.10.order, bf16[128,1024]{1,0:T(8,128)(2,1)} %bitcast.9, ...), custom_call_target="tpu_custom_call" | custom-call | flops 5368709120 | bytes 4194304 | tf_op jit(solution)/shard_map/forward/pallas_call | solution.py:144
  73.0 8.1 %backward.2 = (bf16[1024,128]{1,0:T(8,128)(2,1)}, bf16[1024,128]{1,0:T(8,128)(2,1)}, f32[128,1024]{1,0:T(8,128)}) custom-call(bf16[128,1024]{1,0:T(8,128)(2,1)} %bitcast.10, bf16[128,1024]{1,0:T(8,128)(2,1)} %bitcast.13, f32[8,1024]{1,0:T(8,128)} %get-tuple-element.16.stats_ref, f32[128,1024]{1,0:T(8,128)} %get-tuple-element.17.dq_in, ...), custom_call_target="tpu_custom_call" | custom-call | flops 3758096384 | bytes 4194304 | tf_op jit(solution)/shard_map/backward/pallas_call | solution.py:178
  81.1 2.0 %collective-permute-start.3 = (bf16[1024,128]{1,0:T(8,128)(2,1)}, bf16[1024,128]{1,0:T(8,128)(2,1)S(1)}, u32[]{:S(2)}, u32[]{:S(2)}) collective-permute-start(bf16[1024,128]{1,0:T(8,128)(2,1)} %get-tuple-element.22), channel_id=1, source_target_pairs={{0,8},{8,0},{16,24},{24,16},{32,40},{40,32},{48,56},{56,48},{64,72... | collective-permute-start | bytes 786440 | tf_op jit(solution)/shard_map/ppermute | solution.py:226
  83.2 2.3 %collective-permute-start.4 = (bf16[1024,128]{1,0:T(8,128)(2,1)}, bf16[1024,128]{1,0:T(8,128)(2,1)S(1)}, u32[]{:S(2)}, u32[]{:S(2)}) collective-permute-start(bf16[1024,128]{1,0:T(8,128)(2,1)} %get-tuple-element.24), channel_id=1, source_target_pairs={{0,8},{8,0},{16,24},{24,16},{32,40},{40,32},{48,56},{56,48},{64,72... | collective-permute-start | bytes 786440 | tf_op jit(solution)/shard_map/ppermute | solution.py:227
  85.5 8.2 %backward.3 = (f32[1024,128]{1,0:T(8,128)}, f32[1024,128]{1,0:T(8,128)}, bf16[128,1024]{1,0:T(8,128)(2,1)}) custom-call(bf16[128,1024]{1,0:T(8,128)(2,1)} %bitcast.11, bf16[128,1024]{1,0:T(8,128)(2,1)} %bitcast.14, f32[8,1024]{1,0:T(8,128)} %get-tuple-element.16.stats_ref, f32[128,1024]{1,0:T(8,128)} %get-tuple-element.18.dq_in, ...), custom_call_target="tpu_custom_call" | custom-call | flops 3758096384 | bytes 4194304 | tf_op jit(solution)/shard_map/backward/pallas_call | solution.py:178
  93.6 0.0 collective-permute-done.4
  93.6 1.2 add_convert_fusion.3
  94.8 3.4 %collective-permute-start.5 = (bf16[1024,128]{1,0:T(8,128)(2,1)S(1)}, bf16[1024,128]{1,0:T(8,128)(2,1)S(1)}, u32[]{:S(2)}, u32[]{:S(2)}) collective-permute-start(bf16[1024,128]{1,0:T(8,128)(2,1)S(1)} %add_convert_fusion.3), channel_id=1, source_target_pairs={{0,16},{8,24},{16,0},{24,8},{32,48},{40,56},{48,32},{56,40},{64,80... | collective-permute-start | bytes 786440 | tf_op jit(solution)/shard_map/ppermute | solution.py:228
  98.2 6.9 %all-to-all-start = ((bf16[8,16,256]{2,1,0:T(8,128)(2,1)}), bf16[8,16,256]{2,1,0:T(8,128)(2,1)S(1)}, u32[]{:S(2)}, u32[]{:S(2)}) async-start(bf16[8,16,256]{2,1,0:T(8,128)(2,1)} %bitcast.4), calls=%async_computation | async-start | bytes 131072 | tf_op jit(solution)/shard_map/all_to_all | solution.py:215
  105.1 1.9 %collective-permute-start.7 = (bf16[1024,128]{1,0:T(8,128)(2,1)S(1)}, bf16[1024,128]{1,0:T(8,128)(2,1)S(1)}, u32[]{:S(2)}, u32[]{:S(2)}) collective-permute-start(bf16[1024,128]{1,0:T(8,128)(2,1)S(1)} %copy-done.8), channel_id=1, source_target_pairs={{0,8},{8,0},{16,24},{24,16},{32,40},{40,32},{48,56},{56,48},{64,72... | collective-permute-start | bytes 786440 | tf_op jit(solution)/shard_map/ppermute | solution.py:227
  107.0 0.0 collective-permute-done.3
  107.0 0.8 add_convert_fusion.2
  107.8 3.0 %all-to-all-done = bf16[8,16,256]{2,1,0:T(8,128)(2,1)S(1)} async-done(((bf16[8,16,256]{2,1,0:T(8,128)(2,1)}), bf16[8,16,256]{2,1,0:T(8,128)(2,1)S(1)}, u32[]{:S(2)}, u32[]{:S(2)}) %all-to-all-start) | async-done | bytes 65568 | tf_op jit(solution)/shard_map/all_to_all | solution.py:215
  110.9 6.4 %all-to-all-start.1 = ((bf16[16,64,128]{2,1,0:T(8,128)(2,1)}), bf16[16,64,128]{2,1,0:T(8,128)(2,1)S(1)}, u32[]{:S(2)}, u32[]{:S(2)}) async-start(bf16[16,64,128]{2,1,0:T(8,128)(2,1)} %bitcast.6), calls=%async_computation.1 | async-start | bytes 524288 | tf_op jit(solution)/shard_map/all_to_all | solution.py:230
  117.3 1.9 %collective-permute-start.6 = (bf16[1024,128]{1,0:T(8,128)(2,1)S(1)}, bf16[1024,128]{1,0:T(8,128)(2,1)S(1)}, u32[]{:S(2)}, u32[]{:S(2)}) collective-permute-start(bf16[1024,128]{1,0:T(8,128)(2,1)S(1)} %copy-done.7), channel_id=1, source_target_pairs={{0,8},{8,0},{16,24},{24,16},{32,40},{40,32},{48,56},{56,48},{64,72... | collective-permute-start | bytes 786440 | tf_op jit(solution)/shard_map/ppermute | solution.py:226
  119.3 0.1 add_convert_fusion.1
  119.4 2.3 %collective-permute-start.8 = (bf16[1024,128]{1,0:T(8,128)(2,1)S(1)}, bf16[1024,128]{1,0:T(8,128)(2,1)S(1)}, u32[]{:S(2)}, u32[]{:S(2)}) collective-permute-start(bf16[1024,128]{1,0:T(8,128)(2,1)S(1)} %add_convert_fusion.1), channel_id=1, source_target_pairs={{0,16},{8,24},{16,0},{24,8},{32,48},{40,56},{48,32},{56,40},{64,80... | collective-permute-start | bytes 786440 | tf_op jit(solution)/shard_map/ppermute | solution.py:228
  121.6 8.4 %collective-permute-done.8 = bf16[1024,128]{1,0:T(8,128)(2,1)S(1)} collective-permute-done((bf16[1024,128]{1,0:T(8,128)(2,1)S(1)}, bf16[1024,128]{1,0:T(8,128)(2,1)S(1)}, u32[]{:S(2)}, u32[]{:S(2)}) %collective-permute-start.8) | collective-permute-done | bytes 262176 | tf_op jit(solution)/shard_map/ppermute | solution.py:228
  130.1 0.8 add_convert_fusion
  130.9 3.8 %all-to-all-done.1 = bf16[16,64,128]{2,1,0:T(8,128)(2,1)S(1)} async-done(((bf16[16,64,128]{2,1,0:T(8,128)(2,1)}), bf16[16,64,128]{2,1,0:T(8,128)(2,1)S(1)}, u32[]{:S(2)}, u32[]{:S(2)}) %all-to-all-start.1) | async-done | bytes 262176 | tf_op jit(solution)/shard_map/all_to_all | solution.py:230
  134.7 8.3 %all-to-all-start.2 = ((bf16[16,64,128]{2,1,0:T(8,128)(2,1)}), bf16[16,64,128]{2,1,0:T(8,128)(2,1)S(1)}, u32[]{:S(2)}, u32[]{:S(2)}) async-start(bf16[16,64,128]{2,1,0:T(8,128)(2,1)} %bitcast.7), calls=%async_computation.2 | async-start | bytes 524288 | tf_op jit(solution)/shard_map/all_to_all | solution.py:230
  142.9 0.7 reshape.19
  143.6 17.7 %all-to-all-done.2 = bf16[16,64,128]{2,1,0:T(8,128)(2,1)S(1)} async-done(((bf16[16,64,128]{2,1,0:T(8,128)(2,1)}), bf16[16,64,128]{2,1,0:T(8,128)(2,1)S(1)}, u32[]{:S(2)}, u32[]{:S(2)}) %all-to-all-start.2) | async-done | bytes 262176 | tf_op jit(solution)/shard_map/all_to_all | solution.py:230
  161.4 0.6 pad_maximum_fusion
  (23 shorter events, 0.1 us)
Async XLA Ops:
  39.4 14.9 %copy-start.2 = (bf16[1024,256]{1,0:T(8,128)(2,1)}, bf16[1024,256]{1,0:T(8,128)(2,1)S(1)}, u32[]{:S(2)}) copy-start(bf16[1024,256]{1,0:T(8,128)(2,1)S(1)} %all_gather.3.rest_3_.rest_1_) | copy-start | bytes 1572868
  39.4 11.1 %collective-permute-start.1 = (bf16[1024,256]{1,0:T(8,128)(2,1)S(1)}, bf16[1024,256]{1,0:T(8,128)(2,1)S(1)}, u32[]{:S(2)}, u32[]{:S(2)}) collective-permute-start(bf16[1024,256]{1,0:T(8,128)(2,1)S(1)} %all_gather.3.rest_3_.rest_1_), channel_id=1, source_target_pairs={{0,16},{8,24},{16,0},{24,8},{32,48},{40,56},{48,32},{56,40},{64,80... | collective-permute-start | bytes 1572872 | tf_op jit(solution)/shard_map/ppermute | solution.py:206
  42.8 10.2 %collective-permute-start = (bf16[1024,256]{1,0:T(8,128)(2,1)S(1)}, bf16[1024,256]{1,0:T(8,128)(2,1)S(1)}, u32[]{:S(2)}, u32[]{:S(2)}) collective-permute-start(bf16[1024,256]{1,0:T(8,128)(2,1)S(1)} %all_gather.3.rest_3_.rest_1_), channel_id=1, source_target_pairs={{0,8},{8,0},{16,24},{24,16},{32,40},{40,32},{48,56},{56,48},{64,72... | collective-permute-start | bytes 1572872 | tf_op jit(solution)/shard_map/ppermute | solution.py:207
  50.5 3.8 %copy-start.4 = (bf16[1024,256]{1,0:T(8,128)(2,1)}, bf16[1024,256]{1,0:T(8,128)(2,1)S(1)}, u32[]{:S(2)}) copy-start(bf16[1024,256]{1,0:T(8,128)(2,1)S(1)} %collective-permute-done.1.rest_2_.rest_0_) | copy-start | bytes 1572868
  50.5 3.8 %collective-permute-start.2 = (bf16[1024,256]{1,0:T(8,128)(2,1)S(1)}, bf16[1024,256]{1,0:T(8,128)(2,1)S(1)}, u32[]{:S(2)}, u32[]{:S(2)}) collective-permute-start(bf16[1024,256]{1,0:T(8,128)(2,1)S(1)} %collective-permute-done.1.rest_2_.rest_0_), channel_id=1, source_target_pairs={{0,8},{8,0},{16,24},{24,16},{32,40},{40,32},{48,56},{56,48},{64,72... | collective-permute-start | bytes 1572872 | tf_op jit(solution)/shard_map/ppermute | solution.py:208
  53.1 1.2 copy-start.5
  54.3 0.8 copy-start.6
  81.1 25.9 %collective-permute-start.3 = (bf16[1024,128]{1,0:T(8,128)(2,1)}, bf16[1024,128]{1,0:T(8,128)(2,1)S(1)}, u32[]{:S(2)}, u32[]{:S(2)}) collective-permute-start(bf16[1024,128]{1,0:T(8,128)(2,1)} %get-tuple-element.22), channel_id=1, source_target_pairs={{0,8},{8,0},{16,24},{24,16},{32,40},{40,32},{48,56},{56,48},{64,72... | collective-permute-start | bytes 786440 | tf_op jit(solution)/shard_map/ppermute | solution.py:226
  83.2 10.5 %collective-permute-start.4 = (bf16[1024,128]{1,0:T(8,128)(2,1)}, bf16[1024,128]{1,0:T(8,128)(2,1)S(1)}, u32[]{:S(2)}, u32[]{:S(2)}) collective-permute-start(bf16[1024,128]{1,0:T(8,128)(2,1)} %get-tuple-element.24), channel_id=1, source_target_pairs={{0,8},{8,0},{16,24},{24,16},{32,40},{40,32},{48,56},{56,48},{64,72... | collective-permute-start | bytes 786440 | tf_op jit(solution)/shard_map/ppermute | solution.py:227
  93.6 11.5 %copy-start.8 = (bf16[1024,128]{1,0:T(8,128)(2,1)S(1)}, bf16[1024,128]{1,0:T(8,128)(2,1)}, u32[]{:S(2)}) copy-start(bf16[1024,128]{1,0:T(8,128)(2,1)} %get-tuple-element.28) | copy-start | bytes 786436
  93.6 13.4 %copy-start.3 = (f32[1024,128]{1,0:T(8,128)S(1)}, f32[1024,128]{1,0:T(8,128)}, u32[]{:S(2)}) copy-start(f32[1024,128]{1,0:T(8,128)} %get-tuple-element.21) | copy-start | bytes 1572868
  94.8 12.2 %collective-permute-start.5 = (bf16[1024,128]{1,0:T(8,128)(2,1)S(1)}, bf16[1024,128]{1,0:T(8,128)(2,1)S(1)}, u32[]{:S(2)}, u32[]{:S(2)}) collective-permute-start(bf16[1024,128]{1,0:T(8,128)(2,1)S(1)} %add_convert_fusion.3), channel_id=1, source_target_pairs={{0,16},{8,24},{16,0},{24,8},{32,48},{40,56},{48,32},{56,40},{64,80... | collective-permute-start | bytes 786440 | tf_op jit(solution)/shard_map/ppermute | solution.py:228
  98.2 12.7 %all-to-all-start = ((bf16[8,16,256]{2,1,0:T(8,128)(2,1)}), bf16[8,16,256]{2,1,0:T(8,128)(2,1)S(1)}, u32[]{:S(2)}, u32[]{:S(2)}) async-start(bf16[8,16,256]{2,1,0:T(8,128)(2,1)} %bitcast.4), calls=%async_computation | async-start | bytes 131072 | tf_op jit(solution)/shard_map/all_to_all | solution.py:215
  105.1 14.2 %collective-permute-start.7 = (bf16[1024,128]{1,0:T(8,128)(2,1)S(1)}, bf16[1024,128]{1,0:T(8,128)(2,1)S(1)}, u32[]{:S(2)}, u32[]{:S(2)}) collective-permute-start(bf16[1024,128]{1,0:T(8,128)(2,1)S(1)} %copy-done.8), channel_id=1, source_target_pairs={{0,8},{8,0},{16,24},{24,16},{32,40},{40,32},{48,56},{56,48},{64,72... | collective-permute-start | bytes 786440 | tf_op jit(solution)/shard_map/ppermute | solution.py:227
  107.0 10.3 %copy-start.7 = (bf16[1024,128]{1,0:T(8,128)(2,1)S(1)}, bf16[1024,128]{1,0:T(8,128)(2,1)}, u32[]{:S(2)}) copy-start(bf16[1024,128]{1,0:T(8,128)(2,1)} %get-tuple-element.26) | copy-start | bytes 786436
  107.8 11.4 %copy-start.1 = (f32[1024,128]{1,0:T(8,128)S(1)}, f32[1024,128]{1,0:T(8,128)}, u32[]{:S(2)}) copy-start(f32[1024,128]{1,0:T(8,128)} %get-tuple-element.27) | copy-start | bytes 1572868
  110.9 23.8 %all-to-all-start.1 = ((bf16[16,64,128]{2,1,0:T(8,128)(2,1)}), bf16[16,64,128]{2,1,0:T(8,128)(2,1)S(1)}, u32[]{:S(2)}, u32[]{:S(2)}) async-start(bf16[16,64,128]{2,1,0:T(8,128)(2,1)} %bitcast.6), calls=%async_computation.1 | async-start | bytes 524288 | tf_op jit(solution)/shard_map/all_to_all | solution.py:230
  117.3 4.3 %collective-permute-start.6 = (bf16[1024,128]{1,0:T(8,128)(2,1)S(1)}, bf16[1024,128]{1,0:T(8,128)(2,1)S(1)}, u32[]{:S(2)}, u32[]{:S(2)}) collective-permute-start(bf16[1024,128]{1,0:T(8,128)(2,1)S(1)} %copy-done.7), channel_id=1, source_target_pairs={{0,8},{8,0},{16,24},{24,16},{32,40},{40,32},{48,56},{56,48},{64,72... | collective-permute-start | bytes 786440 | tf_op jit(solution)/shard_map/ppermute | solution.py:226
  119.3 10.8 %copy-start = (f32[1024,128]{1,0:T(8,128)S(1)}, f32[1024,128]{1,0:T(8,128)}, u32[]{:S(2)}) copy-start(f32[1024,128]{1,0:T(8,128)} %get-tuple-element.25) | copy-start | bytes 1572868
  119.4 10.7 %collective-permute-start.8 = (bf16[1024,128]{1,0:T(8,128)(2,1)S(1)}, bf16[1024,128]{1,0:T(8,128)(2,1)S(1)}, u32[]{:S(2)}, u32[]{:S(2)}) collective-permute-start(bf16[1024,128]{1,0:T(8,128)(2,1)S(1)} %add_convert_fusion.1), channel_id=1, source_target_pairs={{0,16},{8,24},{16,0},{24,8},{32,48},{40,56},{48,32},{56,40},{64,80... | collective-permute-start | bytes 786440 | tf_op jit(solution)/shard_map/ppermute | solution.py:228
  134.7 26.7 %all-to-all-start.2 = ((bf16[16,64,128]{2,1,0:T(8,128)(2,1)}), bf16[16,64,128]{2,1,0:T(8,128)(2,1)S(1)}, u32[]{:S(2)}, u32[]{:S(2)}) async-start(bf16[16,64,128]{2,1,0:T(8,128)(2,1)} %bitcast.7), calls=%async_computation.2 | async-start | bytes 524288 | tf_op jit(solution)/shard_map/all_to_all | solution.py:230

commit v2 on v1

v2 whole, which is shorter than its diff:
```python
import functools
import math

import jax
import jax.numpy as jnp
from jax import lax
from jax.experimental import pallas as pl
from jax.experimental.pallas import tpu as pltpu
from jax.sharding import PartitionSpec as P

F32 = jnp.float32
BF16 = jnp.bfloat16
NEG = -1e30
CHUNK = 256
VMEM_LIMIT = 56 * 1024 * 1024


def nt(a, b):
    return lax.dot_general(a, b, (((1,), (1,)), ((), ())), preferred_element_type=F32)


def nn(a, b):
    return lax.dot_general(a, b, (((1,), (0,)), ((), ())), preferred_element_type=F32)


def tn(a, b):
    return lax.dot_general(a, b, (((0,), (0,)), ((), ())), preferred_element_type=F32)


def stack_heads(src, dst, width, group):
    length = src.shape[0]
    for h in range(group):
        dst[h * length:(h + 1) * length, :] = src[:, h * width:(h + 1) * width]


def attention_kernel(
    lengths, order, q_ref, g_ref, own_ref, mine, other,
    send_ref, keep_ref, d_own_ref, dq_ref, p_ref, qr, gr, *, width, group,
):
    length = q_ref.shape[0]
    rows = group * length
    count = mine.shape[0]
    scale = 1.0 / math.sqrt(width)
    rate = scale * math.log2(math.e)
    stack_heads(q_ref, qr, width, group)
    stack_heads(g_ref, gr, width, group)

    tiles = []
    for side, (kv, grads) in enumerate(((other, send_ref), (mine, keep_ref))):
        for at in range(0, count, CHUNK):
            here = pl.ds(at, CHUNK)
            k, v = kv.at[here, pl.ds(0, width)], kv.at[here, pl.ds(width, width)]
            tiles.append((pl.ds(side * count + at, CHUNK), k, v, grads, here))

    def eights(a):
        return a.reshape(a.shape[0] // 8, 8, rows)

    own_k = own_ref[:, :width]
    own_v = own_ref[:, width:]
    slot = lax.rem(lax.broadcasted_iota(jnp.int32, (length, rows), 1), length)
    seen = lax.broadcasted_iota(jnp.int32, (length, rows), 0) <= slot
    s_own = jnp.where(seen, nt(own_k, qr[...]), NEG)
    m = jnp.max(eights(s_own), axis=0)
    for at, k, v, grads, here in tiles:
        s = nt(k[...], qr[...])
        p_ref[at, :] = s
        m = jnp.maximum(m, jnp.max(eights(s), axis=0))
    top = jnp.max(m, axis=0, keepdims=True)

    p_own = jnp.exp2((s_own - top) * rate)
    l = jnp.sum(eights(p_own), axis=0)
    for at, k, v, grads, here in tiles:
        p = jnp.exp2((p_ref[at, :] - top) * rate)
        p_ref[at, :] = p
        l = l + jnp.sum(eights(p), axis=0)
    total = jnp.sum(l, axis=0, keepdims=True)
    live = lengths[order[0]]
    factor = jnp.where(slot[:1] < live, 1.0 / total, 0.0)

    w_own = p_own * factor
    w_own16 = w_own.astype(BF16)
    out = tn(own_v, w_own16)
    for at, k, v, grads, here in tiles:
        w = (p_ref[at, :] * factor).astype(BF16)
        grads[here, width:] = nn(w, gr[...]).astype(grads.dtype)
        out = out + tn(v[...], w)
    delta = jnp.sum(gr[...].T.astype(F32) * out, axis=0, keepdims=True)

    ds_own = (w_own * (nt(own_v, gr[...]) - delta) * scale).astype(BF16)
    d_own_ref[:, :width] = nn(ds_own, qr[...]).astype(BF16)
    d_own_ref[:, width:] = nn(w_own16, gr[...]).astype(BF16)
    dq = tn(own_k, ds_own)
    factor = factor * scale
    for at, k, v, grads, here in tiles:
        ds = (p_ref[at, :] * factor * (nt(v[...], gr[...]) - delta)).astype(BF16)
        grads[here, :width] = nn(ds, qr[...]).astype(grads.dtype)
        dq = dq + tn(k[...], ds)
    for h in range(group):
        part_h = dq[:, h * length:(h + 1) * length]
        dq_ref[:, h * width:(h + 1) * width] = part_h.T.astype(BF16)


VM = pl.BlockSpec(memory_space=pltpu.VMEM)
SM = pl.BlockSpec(memory_space=pltpu.SMEM)


def run_attention(lengths, order, q, g, own, mine, other, width):
    length = q.shape[0]
    group = q.shape[1] // width
    rows = group * length
    count = mine.shape[0]
    return pl.pallas_call(
        functools.partial(attention_kernel, width=width, group=group),
        out_shape=[
            jax.ShapeDtypeStruct((count, 2 * width), BF16),
            jax.ShapeDtypeStruct((count, 2 * width), F32),
            jax.ShapeDtypeStruct((length, 2 * width), BF16),
            jax.ShapeDtypeStruct((length, group * width), BF16),
        ],
        in_specs=[SM, SM] + [VM] * 5,
        out_specs=[VM] * 4,
        scratch_shapes=[
            pltpu.VMEM((2 * count, rows), F32),
            pltpu.VMEM((rows, width), BF16),
            pltpu.VMEM((rows, width), BF16),
        ],
        compiler_params=pltpu.CompilerParams(vmem_limit_bytes=VMEM_LIMIT),
        cost_estimate=pl.CostEstimate(
            flops=24 * count * rows * width, bytes_accessed=1 << 23, transcendentals=0
        ),
        name="attention",
    )(lengths, order, q, g, own, mine, other)


def per_device(query, resp_kv, grad_out, prefix_kv, lengths, order, *, layers, heads):
    width = resp_kv.shape[2] // 2
    shard = prefix_kv.shape[0]
    q, g, own = query[0], grad_out[0], resp_kv[0]
    far = layers // 2
    to_core = [(i, i ^ 1) for i in range(4 * layers)]
    rings = [[4 * (2 * b + a) + i for b in range(far)] for a in range(2) for i in range(4)]
    squares = [[8 * b + 4 * a + 2 * x + c for a in range(2) for x in range(2)] for b in range(far) for c in range(2)]

    def exchange(array, groups):
        return lax.all_to_all(
            array, "roll", split_axis=0, concat_axis=0, tiled=True, axis_index_groups=groups
        )

    def to_all(array, groups):
        copies = len(groups[0])
        sent = jnp.broadcast_to(array[None], (copies,) + array.shape)
        return exchange(sent, groups).reshape(copies * array.shape[0], array.shape[1])

    def total(terms, groups):
        terms = terms.astype(BF16).reshape(len(groups[0]), -1, terms.shape[1])
        return jnp.sum(exchange(terms, groups).astype(F32), axis=0)

    mine = to_all(to_all(prefix_kv, rings), squares)
    other = lax.ppermute(mine, "roll", to_core)

    send, keep, d_own, d_query = run_attention(lengths, order, q, g, own, mine, other, width)
    parts = d_own.reshape(heads, -1, 2 * width)
    parts = lax.all_to_all(parts, "head", split_axis=0, concat_axis=0, tiled=True)
    got = lax.ppermute(send, "roll", to_core)
    terms = (keep + got).astype(BF16)
    terms, parts = lax.optimization_barrier((terms, parts))
    d_resp = jnp.transpose(parts, (1, 0, 2)).reshape(1, parts.shape[1], -1)
    terms = total(terms, squares).astype(BF16)
    return d_query[None], d_resp, total(terms, rings)


def solution(mesh):
    layers = mesh.shape["roll"] // 4
    return jax.shard_map(
        functools.partial(per_device, layers=layers, heads=mesh.shape["head"]),
        mesh=mesh,
        in_specs=(
            P("roll", None, "head"),
            P("roll", None, "head"),
            P("roll", None, "head"),
            P("roll", "head"),
            P(),
            P("roll"),
        ),
        out_specs=(P("roll", None, "head"), P("roll", "head", None), P("roll", "head")),
        check_vma=False,
    )
```

time: 164 us -> 135 us (0.82)
  blocking collectives: 38.8 us -> 64.7 us
  starting transfers between devices: 42.6 us -> 18.4 us
  Pallas kernels: 34.2 us -> 18.2 us
  waiting for transfers between devices: 39.9 us -> 24.7 us
    all_to_all x0 -> x3, blocking collectives: none -> 64.7 us  [exchange(): lax.all_to_all(array, 'roll', split_axis=0, concat_axis=0, tiled=True, ax...]
    all_gather x1 -> x0, blocking collectives: 38.8 us -> none  [per_device(): lax.all_gather(prefix_kv, 'roll', axis=0, tiled=True, axis_index_groups=r...]
    ppermute x9 -> x2, starting transfers between devices: 21 us -> 3.94 us  [the longest x1 2.03 us: per_device(): got = lax.ppermute(send, 'roll', to_core)]
    pallas_call x3 -> x1, Pallas kernels: 34.2 us -> 18.2 us  [run_attention(): pl.pallas_call(functools.partial(attention_kernel, width=width, group=gro...]
    ppermute x9 -> x2, waiting for transfers between devices: 15.4 us -> 1.98 us  [the longest x1 1.98 us: per_device(): other = lax.ppermute(mine, 'roll', to_core)]
    all_to_all x2 -> x1, starting transfers between devices: 14.7 us -> 7.45 us  [exchange(): lax.all_to_all(array, 'roll', split_axis=0, concat_axis=0, tiled=True, ax...]
    all_to_all x2 -> x1, waiting for transfers between devices: 21.4 us -> 18.7 us  [exchange(): lax.all_to_all(array, 'roll', split_axis=0, concat_axis=0, tiled=True, ax...]
  transfers between devices with their start and end apart: 12 -> 4, of which waited for: 6 -> 3; matrix products, arithmetic and copies ran while one was open for 2% -> 2% of each run, Pallas kernels for 5% -> 0%
where the time goes in v2:
time: 135 us; the launch traced here: 133 us
  blocking collectives  64.7 us (48%)
  waiting for transfers between devices  24.7 us (18%)
  starting transfers between devices  18.4 us (14%)
  Pallas kernels  18.2 us (13%)
  other arithmetic  3.38 us (3%)
  local copies, waits for them, and re-layouts  2.52 us (2%)
    all_to_all x3, blocking collectives, exchange(): lax.all_to_all(array, 'roll', split_axis=0, concat_axis=0, tiled=True, ax...  64.7 us
    all_to_all x1, waiting for transfers between devices, exchange(): lax.all_to_all(array, 'roll', split_axis=0, concat_axis=0, tiled=True, ax...  18.7 us
    pallas_call x1, Pallas kernels, run_attention(): pl.pallas_call(functools.partial(attention_kernel, width=width, group=gro...  18.2 us
    all_to_all x1, starting transfers between devices, exchange(): lax.all_to_all(array, 'roll', split_axis=0, concat_axis=0, tiled=True, ax...  7.45 us
    all_to_all x1, starting transfers between devices, per_device(): lax.all_to_all(parts, 'head', split_axis=0, concat_axis=0, tiled=True)  7.04 us
    all_to_all x1, waiting for transfers between devices, per_device(): lax.all_to_all(parts, 'head', split_axis=0, concat_axis=0, tiled=True)  3.96 us
  transfers between devices with their start and end apart: 4, of which 3 were waited for; matrix products, arithmetic and copies ran while one was open for 2% of the time, Pallas kernels for 0%

profile of v2, /device:TPU:24, one launch (start us, length us, event | category | flops | bytes accessed | tf_op | source)
XLA Modules:
  0.0 133.2 jit_solution(1212814660494310447)
XLA Ops:
  0.6 0.8 broadcast_in_dim.16
  1.4 36.3 %all_to_all.25 = bf16[8,64,256]{2,1,0:T(8,128)(2,1)S(1)} all-to-all(bf16[8,64,256]{2,1,0:T(8,128)(2,1)S(1)} %broadcast_in_dim.16), channel_id=1, replica_groups={{0,64,128,192,256,320,384,448},{8,72,136,200,264,328,392,456},{16,80,14..., dimensions={0} | all-to-all | bytes 524288 | tf_op jit(solution)/shard_map/all_to_all | solution.py:145
  37.7 0.1 broadcast_in_dim.18
  37.7 12.5 %all_to_all.26 = bf16[4,512,256]{2,1,0:T(8,128)(2,1)S(1)} all-to-all(bf16[4,512,256]{2,1,0:T(8,128)(2,1)S(1)} %broadcast_in_dim.18), channel_id=1, replica_groups={{0,16,32,48},{8,24,40,56},{64,80,96,112},{72,88,104,120},{128,144,160,1..., dimensions={0} | all-to-all | bytes 2097152 | tf_op jit(solution)/shard_map/all_to_all | solution.py:145
  50.2 0.0 copy-start
  50.2 1.9 %collective-permute-start = (bf16[2048,256]{1,0:T(8,128)(2,1)S(1)}, bf16[2048,256]{1,0:T(8,128)(2,1)S(1)}, u32[]{:S(2)}, u32[]{:S(2)}) collective-permute-start(bf16[2048,256]{1,0:T(8,128)(2,1)S(1)} %bitcast.12), channel_id=1, source_target_pairs={{0,8},{8,0},{16,24},{24,16},{32,40},{40,32},{48,56},{56,48},{64,72... | collective-permute-start | bytes 3145736 | tf_op jit(solution)/shard_map/ppermute | solution.py:159
  52.8 2.0 %collective-permute-done.other = bf16[2048,256]{1,0:T(8,128)(2,1)S(1)} collective-permute-done((bf16[2048,256]{1,0:T(8,128)(2,1)S(1)}, bf16[2048,256]{1,0:T(8,128)(2,1)S(1)}, u32[]{:S(2)}, u32[]{:S(2)}) %collective-permute-start) | collective-permute-done | bytes 1048608 | tf_op jit(solution)/shard_map/ppermute | solution.py:159
  54.8 0.0 copy-start.1
  54.8 0.0 copy-done
  54.8 1.0 copy-done.1
  55.8 18.2 %attention.1 = (bf16[2048,256]{1,0:T(8,128)(2,1)}, f32[2048,256]{1,0:T(8,128)}, bf16[128,256]{1,0:T(8,128)(2,1)}, bf16[128,1024]{1,0:T(8,128)(2,1)}) custom-call(s32[64]{0:T(128)} %lengths.1, s32[1]{0:T(128)S(6)} %copy.11.order, bf16[128,1024]{1,0:T(8,128)(2,1)} %bitcast.16, bf16[128,1024]{1,0:T(8,128)(2,1)} %bitcast.17, bf16[128,256]{1,0:T(8,128)(2,1)} %bitcast.18, ...), custom_call_target="tpu_custom_call" | custom-call | flops 6442450944 | bytes 8388608 | tf_op jit(solution)/shard_map/attention/pallas_call | solution.py:112
  73.9 2.0 %collective-permute-start.1 = (bf16[2048,256]{1,0:T(8,128)(2,1)}, bf16[2048,256]{1,0:T(8,128)(2,1)S(1)}, u32[]{:S(2)}, u32[]{:S(2)}) collective-permute-start(bf16[2048,256]{1,0:T(8,128)(2,1)} %get-tuple-element.11), channel_id=1, source_target_pairs={{0,8},{8,0},{16,24},{24,16},{32,40},{40,32},{48,56},{56,48},{64,72... | collective-permute-start | bytes 3145736 | tf_op jit(solution)/shard_map/ppermute | solution.py:164
  76.0 7.0 %all-to-all-start.2 = ((bf16[8,16,256]{2,1,0:T(8,128)(2,1)}), bf16[8,16,256]{2,1,0:T(8,128)(2,1)S(1)}, u32[]{:S(2)}, u32[]{:S(2)}) async-start(bf16[8,16,256]{2,1,0:T(8,128)(2,1)} %bitcast.15), calls=%async_computation.2 | async-start | bytes 131072 | tf_op jit(solution)/shard_map/all_to_all | solution.py:163
  83.0 0.0 collective-permute-done.1
  83.0 1.8 %add_convert_fusion = bf16[2048,256]{1,0:T(8,128)(2,1)S(1)} fusion(f32[2048,256]{1,0:T(8,128)} %get-tuple-element.10, bf16[2048,256]{1,0:T(8,128)(2,1)S(1)} %collective-permute-done.1), kind=kLoop, calls=%fused_computation | loop fusion | flops 1572864 | bytes 4194304 | tf_op jit(solution)/shard_map/convert_element_type | solution.py:165
  84.8 4.0 %all-to-all-done.2 = bf16[8,16,256]{2,1,0:T(8,128)(2,1)S(1)} async-done(((bf16[8,16,256]{2,1,0:T(8,128)(2,1)}), bf16[8,16,256]{2,1,0:T(8,128)(2,1)S(1)}, u32[]{:S(2)}, u32[]{:S(2)}) %all-to-all-start.2) | async-done | bytes 65568 | tf_op jit(solution)/shard_map/all_to_all | solution.py:163
  88.8 15.9 %all_to_all.27 = bf16[4,512,256]{2,1,0:T(8,128)(2,1)S(1)} all-to-all(bf16[4,512,256]{2,1,0:T(8,128)(2,1)S(1)} %bitcast.10), channel_id=1, replica_groups={{0,16,32,48},{8,24,40,56},{64,80,96,112},{72,88,104,120},{128,144,160,1..., dimensions={0} | all-to-all | bytes 2097152 | tf_op jit(solution)/shard_map/all_to_all | solution.py:145
  104.7 0.9 reduce_sum.21
  105.6 7.5 %all-to-all-start.4 = ((bf16[8,64,256]{2,1,0:T(8,128)(2,1)}), bf16[8,64,256]{2,1,0:T(8,128)(2,1)S(1)}, u32[]{:S(2)}, u32[]{:S(2)}) async-start(bf16[8,64,256]{2,1,0:T(8,128)(2,1)} %bitcast.9), calls=%async_computation.4 | async-start | bytes 524288 | tf_op jit(solution)/shard_map/all_to_all | solution.py:145
  113.1 0.7 reshape.25
  113.8 18.7 %all-to-all-done.4 = bf16[8,64,256]{2,1,0:T(8,128)(2,1)S(1)} async-done(((bf16[8,64,256]{2,1,0:T(8,128)(2,1)}), bf16[8,64,256]{2,1,0:T(8,128)(2,1)S(1)}, u32[]{:S(2)}, u32[]{:S(2)}) %all-to-all-start.4) | async-done | bytes 262176 | tf_op jit(solution)/shard_map/all_to_all | solution.py:145
  132.5 0.7 convert_reduce_fusion
  (1 shorter events, 0.0 us)
Async XLA Ops:
  50.2 4.5 %copy-start = (bf16[4,512,256]{2,1,0:T(8,128)(2,1)}, bf16[4,512,256]{2,1,0:T(8,128)(2,1)S(1)}, u32[]{:S(2)}) copy-start(bf16[4,512,256]{2,1,0:T(8,128)(2,1)S(1)} %all_to_all.26) | copy-start | bytes 3145732
  50.2 4.5 %collective-permute-start = (bf16[2048,256]{1,0:T(8,128)(2,1)S(1)}, bf16[2048,256]{1,0:T(8,128)(2,1)S(1)}, u32[]{:S(2)}, u32[]{:S(2)}) collective-permute-start(bf16[2048,256]{1,0:T(8,128)(2,1)S(1)} %bitcast.12), channel_id=1, source_target_pairs={{0,8},{8,0},{16,24},{24,16},{32,40},{40,32},{48,56},{56,48},{64,72... | collective-permute-start | bytes 3145736 | tf_op jit(solution)/shard_map/ppermute | solution.py:159
  54.8 1.0 copy-start.1
  73.9 9.1 %collective-permute-start.1 = (bf16[2048,256]{1,0:T(8,128)(2,1)}, bf16[2048,256]{1,0:T(8,128)(2,1)S(1)}, u32[]{:S(2)}, u32[]{:S(2)}) collective-permute-start(bf16[2048,256]{1,0:T(8,128)(2,1)} %get-tuple-element.11), channel_id=1, source_target_pairs={{0,8},{8,0},{16,24},{24,16},{32,40},{40,32},{48,56},{56,48},{64,72... | collective-permute-start | bytes 3145736 | tf_op jit(solution)/shard_map/ppermute | solution.py:164
  76.0 12.8 %all-to-all-start.2 = ((bf16[8,16,256]{2,1,0:T(8,128)(2,1)}), bf16[8,16,256]{2,1,0:T(8,128)(2,1)S(1)}, u32[]{:S(2)}, u32[]{:S(2)}) async-start(bf16[8,16,256]{2,1,0:T(8,128)(2,1)} %bitcast.15), calls=%async_computation.2 | async-start | bytes 131072 | tf_op jit(solution)/shard_map/all_to_all | solution.py:163
  105.6 26.9 %all-to-all-start.4 = ((bf16[8,64,256]{2,1,0:T(8,128)(2,1)}), bf16[8,64,256]{2,1,0:T(8,128)(2,1)S(1)}, u32[]{:S(2)}, u32[]{:S(2)}) async-start(bf16[8,64,256]{2,1,0:T(8,128)(2,1)} %bitcast.9), calls=%async_computation.4 | async-start | bytes 524288 | tf_op jit(solution)/shard_map/all_to_all | solution.py:145

commit v3 on v2

--- a/solution.py
+++ b/solution.py
@@ -11,8 +11,8 @@
 F32 = jnp.float32
 BF16 = jnp.bfloat16
 NEG = -1e30
-CHUNK = 256
-VMEM_LIMIT = 56 * 1024 * 1024
+CHUNK = 512
+VMEM_LIMIT = 32 * 1024 * 1024
 
 
 def nt(a, b):
@@ -34,8 +34,8 @@
 
 
 def attention_kernel(
-    lengths, order, q_ref, g_ref, own_ref, mine, other,
-    send_ref, keep_ref, d_own_ref, dq_ref, p_ref, qr, gr, *, width, group,
+    lengths, order, head, q_ref, g_ref, own_ref, mine, other,
+    send_ref, keep_ref, d_own_ref, dq_ref, p_ref, qr, gr, d_own, *, width, group,
 ):
     length = q_ref.shape[0]
     rows = group * length
@@ -87,8 +87,12 @@
     delta = jnp.sum(gr[...].T.astype(F32) * out, axis=0, keepdims=True)
 
     ds_own = (w_own * (nt(own_v, gr[...]) - delta) * scale).astype(BF16)
-    d_own_ref[:, :width] = nn(ds_own, qr[...]).astype(BF16)
-    d_own_ref[:, width:] = nn(w_own16, gr[...]).astype(BF16)
+    d_own[:, :width] = nn(ds_own, qr[...]).astype(BF16)
+    d_own[:, width:] = nn(w_own16, gr[...]).astype(BF16)
+    heads, slots = d_own_ref.shape[:2]
+    for i in range(heads):
+        at = pl.multiple_of((head[0] ^ i) * slots, slots)
+        d_own_ref[i] = d_own[pl.ds(at, slots), :]
     dq = tn(own_k, ds_own)
     factor = factor * scale
     for at, k, v, grads, here in tiles:
@@ -104,7 +108,7 @@
 SM = pl.BlockSpec(memory_space=pltpu.SMEM)
 
 
-def run_attention(lengths, order, q, g, own, mine, other, width):
+def run_attention(lengths, order, head, heads, q, g, own, mine, other, width):
     length = q.shape[0]
     group = q.shape[1] // width
     rows = group * length
@@ -114,22 +118,23 @@
         out_shape=[
             jax.ShapeDtypeStruct((count, 2 * width), BF16),
             jax.ShapeDtypeStruct((count, 2 * width), F32),
-            jax.ShapeDtypeStruct((length, 2 * width), BF16),
+            jax.ShapeDtypeStruct((heads, length // heads, 2 * width), BF16),
             jax.ShapeDtypeStruct((length, group * width), BF16),
         ],
-        in_specs=[SM, SM] + [VM] * 5,
+        in_specs=[SM, SM, SM] + [VM] * 5,
         out_specs=[VM] * 4,
         scratch_shapes=[
             pltpu.VMEM((2 * count, rows), F32),
             pltpu.VMEM((rows, width), BF16),
             pltpu.VMEM((rows, width), BF16),
+            pltpu.VMEM((length, 2 * width), BF16),
         ],
         compiler_params=pltpu.CompilerParams(vmem_limit_bytes=VMEM_LIMIT),
         cost_estimate=pl.CostEstimate(
             flops=24 * count * rows * width, bytes_accessed=1 << 23, transcendentals=0
         ),
         name="attention",
-    )(lengths, order, q, g, own, mine, other)
+    )(lengths, order, head, q, g, own, mine, other)
 
 
 def per_device(query, resp_kv, grad_out, prefix_kv, lengths, order, *, layers, heads):
@@ -158,15 +163,35 @@
     mine = to_all(to_all(prefix_kv, rings), squares)
     other = lax.ppermute(mine, "roll", to_core)
 
-    send, keep, d_own, d_query = run_attention(lengths, order, q, g, own, mine, other, width)
-    parts = d_own.reshape(heads, -1, 2 * width)
-    parts = lax.all_to_all(parts, "head", split_axis=0, concat_axis=0, tiled=True)
+    head = lax.axis_index("head").astype(jnp.int32)
+    send, keep, d_own, d_query = run_attention(
+        lengths, order, head.reshape(1), heads, q, g, own, mine, other, width
+    )
     got = lax.ppermute(send, "roll", to_core)
     terms = (keep + got).astype(BF16)
-    terms, parts = lax.optimization_barrier((terms, parts))
-    d_resp = jnp.transpose(parts, (1, 0, 2)).reshape(1, parts.shape[1], -1)
+    terms, d_own = lax.optimization_barrier((terms, d_own))
+
+    def swap_heads(blocks, bit):
+        sent = [i for i in range(heads) if i & bit]
+        swapped = lax.ppermute(
+            jnp.stack([blocks[i] for i in sent]), "head", [(i, i ^ bit) for i in range(heads)]
+        )
+        return [swapped[sent.index(i)] if i & bit else blocks[i] for i in range(heads)]
+
+    blocks = [d_own[i] for i in range(heads)]
+    bits = [1 << i for i in range(heads.bit_length() - 1)]
+    for bit in bits[:-1]:
+        blocks = swap_heads(blocks, bit)
     terms = total(terms, squares).astype(BF16)
-    return d_query[None], d_resp, total(terms, rings)
+    terms, blocks = lax.optimization_barrier((terms, blocks))
+    blocks = swap_heads(blocks, bits[-1])
+    d_prefix = total(terms, rings)
+
+    for bit in bits:
+        odd = (head & bit) != 0
+        blocks = [jnp.where(odd, blocks[i ^ bit], blocks[i]) for i in range(heads)]
+    d_resp = jnp.concatenate(blocks, axis=1)
+    return d_query[None], d_resp[None], d_prefix
 
 
 def solution(mesh):

time: 135 us -> 130 us (0.963)
  blocking collectives: 64.7 us -> 48.8 us
  waiting for transfers between devices: 24.7 us -> 33.4 us
  starting transfers between devices: 18.4 us -> 25.5 us
  Pallas kernels: 18.2 us -> 16.1 us
  local copies, waits for them, and re-layouts: 2.52 us -> 0.94 us
    all_to_all x3 -> x2, blocking collectives: 64.7 us -> 48.8 us  [exchange(): lax.all_to_all(array, 'roll', split_axis=0, concat_axis=0, tiled=True, ax...]
    ppermute x0 -> x3, starting transfers between devices: none -> 10.6 us  [swap_heads(): lax.ppermute(jnp.stack([blocks[i] for i in sent]), 'head', [(i, i ^ bit)...]
    ppermute x0 -> x3, waiting for transfers between devices: none -> 7.32 us  [swap_heads(): lax.ppermute(jnp.stack([blocks[i] for i in sent]), 'head', [(i, i ^ bit)...]
    all_to_all x1 -> x0, starting transfers between devices: 7.04 us -> none  [per_device(): lax.all_to_all(parts, 'head', split_axis=0, concat_axis=0, tiled=True)]
    all_to_all x1 -> x0, waiting for transfers between devices: 3.96 us -> none  [per_device(): lax.all_to_all(parts, 'head', split_axis=0, concat_axis=0, tiled=True)]
    all_to_all x1 -> x2, starting transfers between devices: 7.45 us -> 11 us  [exchange(): lax.all_to_all(array, 'roll', split_axis=0, concat_axis=0, tiled=True, ax...]
    all_to_all x1 -> x2, waiting for transfers between devices: 18.7 us -> 21.6 us  [exchange(): lax.all_to_all(array, 'roll', split_axis=0, concat_axis=0, tiled=True, ax...]
    ppermute x1, waiting for transfers between devices: 0.01 us -> 2.51 us  [per_device(): got = lax.ppermute(send, 'roll', to_core)]
  transfers between devices with their start and end apart: 4 -> 7, of which waited for: 3 -> 6; matrix products, arithmetic and copies ran while one was open for 2% -> 0% of each run, Pallas kernels for 0% -> 0%
where the time goes in v3:
time: 130 us; the launch traced here: 129 us
  blocking collectives  48.8 us (38%)
  waiting for transfers between devices  33.4 us (26%)
  starting transfers between devices  25.5 us (20%)
  Pallas kernels  16.1 us (12%)
  other arithmetic  2.99 us (2%)
  between operations  1.48 us (1%)
    all_to_all x2, blocking collectives, exchange(): lax.all_to_all(array, 'roll', split_axis=0, concat_axis=0, tiled=True, ax...  48.8 us
    all_to_all x2, waiting for transfers between devices, exchange(): lax.all_to_all(array, 'roll', split_axis=0, concat_axis=0, tiled=True, ax...  21.6 us
    pallas_call x1, Pallas kernels, run_attention(): pl.pallas_call(functools.partial(attention_kernel, width=width, group=gro...  16.1 us
    all_to_all x2, starting transfers between devices, exchange(): lax.all_to_all(array, 'roll', split_axis=0, concat_axis=0, tiled=True, ax...  11 us
    ppermute x3, starting transfers between devices, swap_heads(): lax.ppermute(jnp.stack([blocks[i] for i in sent]), 'head', [(i, i ^ bit)...  10.6 us
    ppermute x3, waiting for transfers between devices, swap_heads(): lax.ppermute(jnp.stack([blocks[i] for i in sent]), 'head', [(i, i ^ bit)...  7.32 us
  transfers between devices with their start and end apart: 7, of which 6 were waited for; matrix products, arithmetic and copies ran while one was open for 0% of the time, Pallas kernels for 0%

profile of v3, /device:TPU:24, one launch (start us, length us, event | category | flops | bytes accessed | tf_op | source)
XLA Modules:
  0.0 129.2 jit_solution(15950848485927289545)
XLA Ops:
  0.6 0.0 copy-start
  0.6 0.0 copy-start.1
  0.7 0.0 copy-start.2
  0.7 0.0 copy-start.3
  0.7 0.8 broadcast_in_dim.19
  1.5 36.3 %all_to_all.20 = bf16[8,64,256]{2,1,0:T(8,128)(2,1)S(1)} all-to-all(bf16[8,64,256]{2,1,0:T(8,128)(2,1)S(1)} %broadcast_in_dim.19), channel_id=1, replica_groups={{0,64,128,192,256,320,384,448},{8,72,136,200,264,328,392,456},{16,80,14..., dimensions={0} | all-to-all | bytes 524288 | tf_op jit(solution)/shard_map/all_to_all | solution.py:150
  37.8 0.1 broadcast_in_dim.21
  37.8 12.5 %all_to_all.21 = bf16[4,512,256]{2,1,0:T(8,128)(2,1)S(1)} all-to-all(bf16[4,512,256]{2,1,0:T(8,128)(2,1)S(1)} %broadcast_in_dim.21), channel_id=1, replica_groups={{0,16,32,48},{8,24,40,56},{64,80,96,112},{72,88,104,120},{128,144,160,1..., dimensions={0} | all-to-all | bytes 2097152 | tf_op jit(solution)/shard_map/all_to_all | solution.py:150
  50.3 1.9 %collective-permute-start = (bf16[2048,256]{1,0:T(8,128)(2,1)S(1)}, bf16[2048,256]{1,0:T(8,128)(2,1)S(1)}, u32[]{:S(2)}, u32[]{:S(2)}) collective-permute-start(bf16[2048,256]{1,0:T(8,128)(2,1)S(1)} %bitcast.58), channel_id=1, source_target_pairs={{0,8},{8,0},{16,24},{24,16},{32,40},{40,32},{48,56},{56,48},{64,72... | collective-permute-start | bytes 3145736 | tf_op jit(solution)/shard_map/ppermute | solution.py:164
  52.9 2.0 %collective-permute-done.other = bf16[2048,256]{1,0:T(8,128)(2,1)S(1)} collective-permute-done((bf16[2048,256]{1,0:T(8,128)(2,1)S(1)}, bf16[2048,256]{1,0:T(8,128)(2,1)S(1)}, u32[]{:S(2)}, u32[]{:S(2)}) %collective-permute-start) | collective-permute-done | bytes 1048608 | tf_op jit(solution)/shard_map/ppermute | solution.py:164
  54.9 0.0 copy-done
  54.9 0.0 copy-done.1
  54.9 0.0 copy-done.2
  54.9 0.0 copy-done.3
  54.9 16.1 %attention.1 = (bf16[2048,256]{1,0:T(8,128)(2,1)S(1)}, f32[2048,256]{1,0:T(8,128)S(1)}, bf16[8,16,256]{2,1,0:T(8,128)(2,1)S(1)}, bf16[128,1024]{1,0:T(8,128)(2,1)}) custom-call(s32[64]{0:T(128)S(1)} %copy-done.3, s32[1]{0:T(128)S(6)} %copy.16.order, s32[1]{0:T(128)} %bitcast.head, bf16[128,1024]{1,0:T(8,128)(2,1)S(1)} %bitcast.60, ...), custom_call_target="tpu_custom_call" | custom-call | flops 6442450944 | bytes 8388608 | tf_op jit(solution)/shard_map/attention/pallas_call | solution.py:116
  71.0 2.0 %collective-permute-start.1 = (bf16[2048,256]{1,0:T(8,128)(2,1)S(1)}, bf16[2048,256]{1,0:T(8,128)(2,1)S(1)}, u32[]{:S(2)}, u32[]{:S(2)}) collective-permute-start(bf16[2048,256]{1,0:T(8,128)(2,1)S(1)} %get-tuple-element.20), channel_id=1, source_target_pairs={{0,8},{8,0},{16,24},{24,16},{32,40},{40,32},{48,56},{56,48},{64,72... | collective-permute-start | bytes 3145736 | tf_op jit(solution)/shard_map/ppermute | solution.py:170
  73.1 2.5 %collective-permute-done.1 = bf16[2048,256]{1,0:T(8,128)(2,1)S(1)} collective-permute-done((bf16[2048,256]{1,0:T(8,128)(2,1)S(1)}, bf16[2048,256]{1,0:T(8,128)(2,1)S(1)}, u32[]{:S(2)}, u32[]{:S(2)}) %collective-permute-start.1) | collective-permute-done | bytes 1048608 | tf_op jit(solution)/shard_map/ppermute | solution.py:170
  75.6 1.3 %add_convert_fusion = bf16[2048,256]{1,0:T(8,128)(2,1)} fusion(f32[2048,256]{1,0:T(8,128)S(1)} %get-tuple-element.19, bf16[2048,256]{1,0:T(8,128)(2,1)S(1)} %collective-permute-done.1), kind=kLoop, calls=%fused_computation | loop fusion | flops 1572864 | bytes 4194304 | tf_op jit(solution)/shard_map/convert_element_type | solution.py:171
  76.9 3.5 %all-to-all-start.2 = ((bf16[4,512,256]{2,1,0:T(8,128)(2,1)}), bf16[4,512,256]{2,1,0:T(8,128)(2,1)S(1)}, u32[]{:S(2)}, u32[]{:S(2)}) async-start(bf16[4,512,256]{2,1,0:T(8,128)(2,1)} %bitcast.7), calls=%async_computation.2 | async-start | bytes 2097152 | tf_op jit(solution)/shard_map/all_to_all | solution.py:150
  80.4 2.7 %collective-permute-start.2 = (bf16[4,16,256]{2,1,0:T(8,128)(2,1)S(1)}, bf16[4,16,256]{2,1,0:T(8,128)(2,1)S(1)}, u32[]{:S(2)}, u32[]{:S(2)}) collective-permute-start(bf16[4,16,256]{2,1,0:T(8,128)(2,1)S(1)} %pad_maximum_fusion), channel_id=1, source_target_pairs={{0,1},{1,0},{2,3},{3,2},{4,5},{5,4},{6,7},{7,6},{8,9},{9,8},{10,11... | collective-permute-start | bytes 98312 | tf_op jit(solution)/shard_map/ppermute | solution.py:176
  83.1 3.1 %collective-permute-done.2 = bf16[4,16,256]{2,1,0:T(8,128)(2,1)S(1)} collective-permute-done((bf16[4,16,256]{2,1,0:T(8,128)(2,1)S(1)}, bf16[4,16,256]{2,1,0:T(8,128)(2,1)S(1)}, u32[]{:S(2)}, u32[]{:S(2)}) %collective-permute-start.2) | collective-permute-done | bytes 32800 | tf_op jit(solution)/shard_map/ppermute | solution.py:176
  86.3 3.1 %collective-permute-start.3 = (bf16[4,16,256]{2,1,0:T(8,128)(2,1)S(1)}, bf16[4,16,256]{2,1,0:T(8,128)(2,1)S(1)}, u32[]{:S(2)}, u32[]{:S(2)}) collective-permute-start(bf16[4,16,256]{2,1,0:T(8,128)(2,1)S(1)} %pad_maximum_fusion.1), channel_id=1, source_target_pairs={{0,2},{1,3},{2,0},{3,1},{4,6},{5,7},{6,4},{7,5},{8,10},{9,11},{10,... | collective-permute-start | bytes 98312 | tf_op jit(solution)/shard_map/ppermute | solution.py:176
  89.4 4.2 %collective-permute-done.3 = bf16[4,16,256]{2,1,0:T(8,128)(2,1)S(1)} collective-permute-done((bf16[4,16,256]{2,1,0:T(8,128)(2,1)S(1)}, bf16[4,16,256]{2,1,0:T(8,128)(2,1)S(1)}, u32[]{:S(2)}, u32[]{:S(2)}) %collective-permute-start.3) | collective-permute-done | bytes 32800 | tf_op jit(solution)/shard_map/ppermute | solution.py:176
  93.6 1.0 all-to-all-done.2
  94.6 0.9 reduce_sum.21
  95.5 4.8 %collective-permute-start.4 = (bf16[4,16,256]{2,1,0:T(8,128)(2,1)S(1)}, bf16[4,16,256]{2,1,0:T(8,128)(2,1)S(1)}, u32[]{:S(2)}, u32[]{:S(2)}) collective-permute-start(bf16[4,16,256]{2,1,0:T(8,128)(2,1)S(1)} %pad_maximum_fusion.2), channel_id=1, source_target_pairs={{0,4},{1,5},{2,6},{3,7},{4,0},{5,1},{6,2},{7,3},{8,12},{9,13},{10,... | collective-permute-start | bytes 98312 | tf_op jit(solution)/shard_map/ppermute | solution.py:176
  100.3 7.5 %all-to-all-start.3 = ((bf16[8,64,256]{2,1,0:T(8,128)(2,1)}), bf16[8,64,256]{2,1,0:T(8,128)(2,1)S(1)}, u32[]{:S(2)}, u32[]{:S(2)}) async-start(bf16[8,64,256]{2,1,0:T(8,128)(2,1)} %bitcast.25), calls=%async_computation.3 | async-start | bytes 524288 | tf_op jit(solution)/shard_map/all_to_all | solution.py:150
  107.8 0.0 collective-permute-done.4
  107.9 0.0 copy-start.4
  107.9 20.6 %all-to-all-done.3 = bf16[8,64,256]{2,1,0:T(8,128)(2,1)S(1)} async-done(((bf16[8,64,256]{2,1,0:T(8,128)(2,1)}), bf16[8,64,256]{2,1,0:T(8,128)(2,1)S(1)}, u32[]{:S(2)}, u32[]{:S(2)}) %all-to-all-start.3) | async-done | bytes 262176 | tf_op jit(solution)/shard_map/all_to_all | solution.py:150
  128.5 0.7 convert_reduce_fusion
  129.2 0.0 copy-done.4
  (14 shorter events, 0.1 us)
Async XLA Ops:
  0.6 54.2 %copy-start = (bf16[1,128,1024]{2,1,0:T(8,128)(2,1)S(1)}, bf16[1,128,1024]{2,1,0:T(8,128)(2,1)}, u32[]{:S(2)}) copy-start(bf16[1,128,1024]{2,1,0:T(8,128)(2,1)} %param.6) | copy-start | bytes 786436
  0.6 54.2 %copy-start.1 = (bf16[1,128,1024]{2,1,0:T(8,128)(2,1)S(1)}, bf16[1,128,1024]{2,1,0:T(8,128)(2,1)}, u32[]{:S(2)}) copy-start(bf16[1,128,1024]{2,1,0:T(8,128)(2,1)} %param.8) | copy-start | bytes 786436
  0.7 54.2 %copy-start.2 = (bf16[1,128,256]{2,1,0:T(8,128)(2,1)S(1)}, bf16[1,128,256]{2,1,0:T(8,128)(2,1)}, u32[]{:S(2)}) copy-start(bf16[1,128,256]{2,1,0:T(8,128)(2,1)} %param.7) | copy-start | bytes 196612
  0.7 54.2 %copy-start.3 = (s32[64]{0:T(128)S(1)}, s32[64]{0:T(128)}, u32[]{:S(2)}) copy-start(s32[64]{0:T(128)} %lengths.1) | copy-start | bytes 772
  50.3 4.5 %collective-permute-start = (bf16[2048,256]{1,0:T(8,128)(2,1)S(1)}, bf16[2048,256]{1,0:T(8,128)(2,1)S(1)}, u32[]{:S(2)}, u32[]{:S(2)}) collective-permute-start(bf16[2048,256]{1,0:T(8,128)(2,1)S(1)} %bitcast.58), channel_id=1, source_target_pairs={{0,8},{8,0},{16,24},{24,16},{32,40},{40,32},{48,56},{56,48},{64,72... | collective-permute-start | bytes 3145736 | tf_op jit(solution)/shard_map/ppermute | solution.py:164
  71.0 4.5 %collective-permute-start.1 = (bf16[2048,256]{1,0:T(8,128)(2,1)S(1)}, bf16[2048,256]{1,0:T(8,128)(2,1)S(1)}, u32[]{:S(2)}, u32[]{:S(2)}) collective-permute-start(bf16[2048,256]{1,0:T(8,128)(2,1)S(1)} %get-tuple-element.20), channel_id=1, source_target_pairs={{0,8},{8,0},{16,24},{24,16},{32,40},{40,32},{48,56},{56,48},{64,72... | collective-permute-start | bytes 3145736 | tf_op jit(solution)/shard_map/ppermute | solution.py:170
  76.9 17.7 %all-to-all-start.2 = ((bf16[4,512,256]{2,1,0:T(8,128)(2,1)}), bf16[4,512,256]{2,1,0:T(8,128)(2,1)S(1)}, u32[]{:S(2)}, u32[]{:S(2)}) async-start(bf16[4,512,256]{2,1,0:T(8,128)(2,1)} %bitcast.7), calls=%async_computation.2 | async-start | bytes 2097152 | tf_op jit(solution)/shard_map/all_to_all | solution.py:150
  80.4 5.8 %collective-permute-start.2 = (bf16[4,16,256]{2,1,0:T(8,128)(2,1)S(1)}, bf16[4,16,256]{2,1,0:T(8,128)(2,1)S(1)}, u32[]{:S(2)}, u32[]{:S(2)}) collective-permute-start(bf16[4,16,256]{2,1,0:T(8,128)(2,1)S(1)} %pad_maximum_fusion), channel_id=1, source_target_pairs={{0,1},{1,0},{2,3},{3,2},{4,5},{5,4},{6,7},{7,6},{8,9},{9,8},{10,11... | collective-permute-start | bytes 98312 | tf_op jit(solution)/shard_map/ppermute | solution.py:176
  86.3 7.3 %collective-permute-start.3 = (bf16[4,16,256]{2,1,0:T(8,128)(2,1)S(1)}, bf16[4,16,256]{2,1,0:T(8,128)(2,1)S(1)}, u32[]{:S(2)}, u32[]{:S(2)}) collective-permute-start(bf16[4,16,256]{2,1,0:T(8,128)(2,1)S(1)} %pad_maximum_fusion.1), channel_id=1, source_target_pairs={{0,2},{1,3},{2,0},{3,1},{4,6},{5,7},{6,4},{7,5},{8,10},{9,11},{10,... | collective-permute-start | bytes 98312 | tf_op jit(solution)/shard_map/ppermute | solution.py:176
  95.5 12.3 %collective-permute-start.4 = (bf16[4,16,256]{2,1,0:T(8,128)(2,1)S(1)}, bf16[4,16,256]{2,1,0:T(8,128)(2,1)S(1)}, u32[]{:S(2)}, u32[]{:S(2)}) collective-permute-start(bf16[4,16,256]{2,1,0:T(8,128)(2,1)S(1)} %pad_maximum_fusion.2), channel_id=1, source_target_pairs={{0,4},{1,5},{2,6},{3,7},{4,0},{5,1},{6,2},{7,3},{8,12},{9,13},{10,... | collective-permute-start | bytes 98312 | tf_op jit(solution)/shard_map/ppermute | solution.py:176
  100.3 28.3 %all-to-all-start.3 = ((bf16[8,64,256]{2,1,0:T(8,128)(2,1)}), bf16[8,64,256]{2,1,0:T(8,128)(2,1)S(1)}, u32[]{:S(2)}, u32[]{:S(2)}) async-start(bf16[8,64,256]{2,1,0:T(8,128)(2,1)} %bitcast.25), calls=%async_computation.3 | async-start | bytes 524288 | tf_op jit(solution)/shard_map/all_to_all | solution.py:150
  107.9 21.3 %copy-start.4 = (bf16[16,2048]{1,0:T(8,128)(2,1)}, bf16[16,2048]{1,0:T(8,128)(2,1)S(1)}, u32[]{:S(2)}) copy-start(bf16[16,2048]{1,0:T(8,128)(2,1)S(1)} %constant_dynamic-update-slice_fusion) | copy-start | bytes 196612

commit v4 on v3

--- a/solution.py
+++ b/solution.py
@@ -27,24 +27,15 @@
     return lax.dot_general(a, b, (((0,), (0,)), ((), ())), preferred_element_type=F32)
 
 
-def stack_heads(src, dst, width, group):
-    length = src.shape[0]
-    for h in range(group):
-        dst[h * length:(h + 1) * length, :] = src[:, h * width:(h + 1) * width]
-
-
 def attention_kernel(
-    lengths, order, head, q_ref, g_ref, own_ref, mine, other,
-    send_ref, keep_ref, d_own_ref, dq_ref, p_ref, qr, gr, d_own, *, width, group,
+    lengths, order, head, qr, gr, own_ref, mine, other,
+    send_ref, keep_ref, d_own_ref, dq_ref, p_ref, d_own, *, width, group,
 ):
-    length = q_ref.shape[0]
-    rows = group * length
+    rows = qr.shape[0]
+    length = rows // group
     count = mine.shape[0]
     scale = 1.0 / math.sqrt(width)
     rate = scale * math.log2(math.e)
-    stack_heads(q_ref, qr, width, group)
-    stack_heads(g_ref, gr, width, group)
-
     tiles = []
     for side, (kv, grads) in enumerate(((other, send_ref), (mine, keep_ref))):
         for at in range(0, count, CHUNK):
@@ -109,9 +100,9 @@
 
 
 def run_attention(lengths, order, head, heads, q, g, own, mine, other, width):
-    length = q.shape[0]
-    group = q.shape[1] // width
-    rows = group * length
+    rows = q.shape[0]
+    length = own.shape[0]
+    group = rows // length
     count = mine.shape[0]
     return pl.pallas_call(
         functools.partial(attention_kernel, width=width, group=group),
@@ -125,8 +116,6 @@
         out_specs=[VM] * 4,
         scratch_shapes=[
             pltpu.VMEM((2 * count, rows), F32),
-            pltpu.VMEM((rows, width), BF16),
-            pltpu.VMEM((rows, width), BF16),
             pltpu.VMEM((length, 2 * width), BF16),
         ],
         compiler_params=pltpu.CompilerParams(vmem_limit_bytes=VMEM_LIMIT),
@@ -140,7 +129,13 @@
 def per_device(query, resp_kv, grad_out, prefix_kv, lengths, order, *, layers, heads):
     width = resp_kv.shape[2] // 2
     shard = prefix_kv.shape[0]
-    q, g, own = query[0], grad_out[0], resp_kv[0]
+    own = resp_kv[0]
+    length = own.shape[0]
+
+    def stack_heads(a):
+        return jnp.transpose(a[0].reshape(length, -1, width), (1, 0, 2)).reshape(-1, width)
+
+    q, g = stack_heads(query), stack_heads(grad_out)
     far = layers // 2
     to_core = [(i, i ^ 1) for i in range(4 * layers)]
     rings = [[4 * (2 * b + a) + i for b in range(far)] for a in range(2) for i in range(4)]
@@ -156,9 +151,11 @@
         sent = jnp.broadcast_to(array[None], (copies,) + array.shape)
         return exchange(sent, groups).reshape(copies * array.shape[0], array.shape[1])
 
-    def total(terms, groups):
-        terms = terms.astype(BF16).reshape(len(groups[0]), -1, terms.shape[1])
-        return jnp.sum(exchange(terms, groups).astype(F32), axis=0)
+    def terms_of_all(terms, groups):
+        return exchange(terms.astype(BF16).reshape(len(groups[0]), -1, terms.shape[1]), groups)
+
+    def total(terms):
+        return jnp.sum(terms.astype(F32), axis=0)
 
     mine = to_all(to_all(prefix_kv, rings), squares)
     other = lax.ppermute(mine, "roll", to_core)
@@ -182,10 +179,12 @@
     bits = [1 << i for i in range(heads.bit_length() - 1)]
     for bit in bits[:-1]:
         blocks = swap_heads(blocks, bit)
-    terms = total(terms, squares).astype(BF16)
+    terms = total(terms_of_all(terms, squares)).astype(BF16)
     terms, blocks = lax.optimization_barrier((terms, blocks))
     blocks = swap_heads(blocks, bits[-1])
-    d_prefix = total(terms, rings)
+    terms = terms_of_all(terms, rings)
+    terms, blocks = lax.optimization_barrier((terms, blocks))
+    d_prefix = total(terms)
 
     for bit in bits:
         odd = (head & bit) != 0

time: 130 us -> 125 us (0.962)
  waiting for transfers between devices: 33.4 us -> 28.8 us
    all_to_all x2, waiting for transfers between devices: 21.6 us -> 14.6 us  [exchange(): lax.all_to_all(array, 'roll', split_axis=0, concat_axis=0, tiled=True, ax...]
    ppermute x3, waiting for transfers between devices: 7.32 us -> 9.96 us  [swap_heads(): lax.ppermute(jnp.stack([blocks[i] for i in sent]), 'head', [(i, i ^ bit)...]
  transfers between devices with their start and end apart: 7 -> 7, of which waited for: 6 -> 7; matrix products, arithmetic and copies ran while one was open for 0% -> 0% of each run, Pallas kernels for 0% -> 0%
where the time goes in v4:
time: 125 us
  blocking collectives  48.9 us (39%)
  waiting for transfers between devices  28.8 us (23%)
  starting transfers between devices  25.5 us (20%)
  Pallas kernels  16.2 us (13%)
  other arithmetic  2.98 us (2%)
  between operations  1.51 us (1%)
    all_to_all x2, blocking collectives, exchange(): lax.all_to_all(array, 'roll', split_axis=0, concat_axis=0, tiled=True, ax...  48.9 us
    pallas_call x1, Pallas kernels, run_attention(): pl.pallas_call(functools.partial(attention_kernel, width=width, group=gro...  16.2 us
    all_to_all x2, waiting for transfers between devices, exchange(): lax.all_to_all(array, 'roll', split_axis=0, concat_axis=0, tiled=True, ax...  14.6 us
    all_to_all x2, starting transfers between devices, exchange(): lax.all_to_all(array, 'roll', split_axis=0, concat_axis=0, tiled=True, ax...  11.1 us
    ppermute x3, starting transfers between devices, swap_heads(): lax.ppermute(jnp.stack([blocks[i] for i in sent]), 'head', [(i, i ^ bit)...  10.4 us
    ppermute x3, waiting for transfers between devices, swap_heads(): lax.ppermute(jnp.stack([blocks[i] for i in sent]), 'head', [(i, i ^ bit)...  9.96 us
    ppermute x1, waiting for transfers between devices, per_device(): got = lax.ppermute(send, 'roll', to_core)  2.51 us
  transfers between devices with their start and end apart: 7, of which 7 were waited for; matrix products, arithmetic and copies ran while one was open for 0% of the time, Pallas kernels for 0%

profile of v4, /device:TPU:24, one launch (start us, length us, event | category | flops | bytes accessed | tf_op | source)
XLA Modules:
  0.0 125.0 jit_solution(5449670713284116500)
XLA Ops:
  0.6 0.0 copy-start.2
  0.6 0.8 broadcast_in_dim.19
  1.5 36.3 %all_to_all.20 = bf16[8,64,256]{2,1,0:T(8,128)(2,1)S(1)} all-to-all(bf16[8,64,256]{2,1,0:T(8,128)(2,1)S(1)} %broadcast_in_dim.19), channel_id=1, replica_groups={{0,64,128,192,256,320,384,448},{8,72,136,200,264,328,392,456},{16,80,14..., dimensions={0} | all-to-all | bytes 524288 | tf_op jit(solution)/shard_map/all_to_all | solution.py:145
  37.7 0.0 copy-start.3
  37.7 0.1 broadcast_in_dim.21
  37.8 0.0 copy-start
  37.8 0.0 copy-start.1
  37.8 12.6 %all_to_all.21 = bf16[4,512,256]{2,1,0:T(8,128)(2,1)S(1)} all-to-all(bf16[4,512,256]{2,1,0:T(8,128)(2,1)S(1)} %broadcast_in_dim.21), channel_id=1, replica_groups={{0,16,32,48},{8,24,40,56},{64,80,96,112},{72,88,104,120},{128,144,160,1..., dimensions={0} | all-to-all | bytes 2097152 | tf_op jit(solution)/shard_map/all_to_all | solution.py:145
  50.4 1.9 %collective-permute-start = (bf16[2048,256]{1,0:T(8,128)(2,1)S(1)}, bf16[2048,256]{1,0:T(8,128)(2,1)S(1)}, u32[]{:S(2)}, u32[]{:S(2)}) collective-permute-start(bf16[2048,256]{1,0:T(8,128)(2,1)S(1)} %bitcast.48), channel_id=1, source_target_pairs={{0,8},{8,0},{16,24},{24,16},{32,40},{40,32},{48,56},{56,48},{64,72... | collective-permute-start | bytes 3145736 | tf_op jit(solution)/shard_map/ppermute | solution.py:161
  52.4 0.0 copy-done.2
  52.5 0.0 copy-done.3
  53.2 1.8 %collective-permute-done.other = bf16[2048,256]{1,0:T(8,128)(2,1)S(1)} collective-permute-done((bf16[2048,256]{1,0:T(8,128)(2,1)S(1)}, bf16[2048,256]{1,0:T(8,128)(2,1)S(1)}, u32[]{:S(2)}, u32[]{:S(2)}) %collective-permute-start) | collective-permute-done | bytes 1048608 | tf_op jit(solution)/shard_map/ppermute | solution.py:161
  55.0 0.0 copy-done
  55.0 0.0 copy-done.1
  55.0 16.2 %attention.1 = (bf16[2048,256]{1,0:T(8,128)(2,1)S(1)}, f32[2048,256]{1,0:T(8,128)S(1)}, bf16[8,16,256]{2,1,0:T(8,128)(2,1)S(1)}, bf16[128,1024]{1,0:T(8,128)(2,1)}) custom-call(s32[64]{0:T(128)S(1)} %copy-done.1, s32[1]{0:T(128)S(6)} %copy.22.order, s32[1]{0:T(128)} %bitcast.head, bf16[1024,128]{1,0:T(8,128)(2,1)S(1)} %bitcast.50, ...), custom_call_target="tpu_custom_call" | custom-call | flops 6442450944 | bytes 8388608 | tf_op jit(solution)/shard_map/attention/pallas_call | solution.py:107
  71.2 2.0 %collective-permute-start.1 = (bf16[2048,256]{1,0:T(8,128)(2,1)S(1)}, bf16[2048,256]{1,0:T(8,128)(2,1)S(1)}, u32[]{:S(2)}, u32[]{:S(2)}) collective-permute-start(bf16[2048,256]{1,0:T(8,128)(2,1)S(1)} %get-tuple-element.29), channel_id=1, source_target_pairs={{0,8},{8,0},{16,24},{24,16},{32,40},{40,32},{48,56},{56,48},{64,72... | collective-permute-start | bytes 3145736 | tf_op jit(solution)/shard_map/ppermute | solution.py:167
  73.2 2.5 %collective-permute-done.1 = bf16[2048,256]{1,0:T(8,128)(2,1)S(1)} collective-permute-done((bf16[2048,256]{1,0:T(8,128)(2,1)S(1)}, bf16[2048,256]{1,0:T(8,128)(2,1)S(1)}, u32[]{:S(2)}, u32[]{:S(2)}) %collective-permute-start.1) | collective-permute-done | bytes 1048608 | tf_op jit(solution)/shard_map/ppermute | solution.py:167
  75.7 1.3 %add_convert_fusion = bf16[2048,256]{1,0:T(8,128)(2,1)} fusion(f32[2048,256]{1,0:T(8,128)S(1)} %get-tuple-element.28, bf16[2048,256]{1,0:T(8,128)(2,1)S(1)} %collective-permute-done.1), kind=kLoop, calls=%fused_computation | loop fusion | flops 1572864 | bytes 4194304 | tf_op jit(solution)/shard_map/convert_element_type | solution.py:168
  77.0 3.5 %all-to-all-start.2 = ((bf16[4,512,256]{2,1,0:T(8,128)(2,1)}), bf16[4,512,256]{2,1,0:T(8,128)(2,1)S(1)}, u32[]{:S(2)}, u32[]{:S(2)}) async-start(bf16[4,512,256]{2,1,0:T(8,128)(2,1)} %bitcast.9), calls=%async_computation.2 | async-start | bytes 2097152 | tf_op jit(solution)/shard_map/all_to_all | solution.py:145
  80.6 2.7 %collective-permute-start.2 = (bf16[4,16,256]{2,1,0:T(8,128)(2,1)S(1)}, bf16[4,16,256]{2,1,0:T(8,128)(2,1)S(1)}, u32[]{:S(2)}, u32[]{:S(2)}) collective-permute-start(bf16[4,16,256]{2,1,0:T(8,128)(2,1)S(1)} %pad_maximum_fusion), channel_id=1, source_target_pairs={{0,1},{1,0},{2,3},{3,2},{4,5},{5,4},{6,7},{7,6},{8,9},{9,8},{10,11... | collective-permute-start | bytes 98312 | tf_op jit(solution)/shard_map/ppermute | solution.py:173
  83.2 3.1 %collective-permute-done.2 = bf16[4,16,256]{2,1,0:T(8,128)(2,1)S(1)} collective-permute-done((bf16[4,16,256]{2,1,0:T(8,128)(2,1)S(1)}, bf16[4,16,256]{2,1,0:T(8,128)(2,1)S(1)}, u32[]{:S(2)}, u32[]{:S(2)}) %collective-permute-start.2) | collective-permute-done | bytes 32800 | tf_op jit(solution)/shard_map/ppermute | solution.py:173
  86.4 3.1 %collective-permute-start.3 = (bf16[4,16,256]{2,1,0:T(8,128)(2,1)S(1)}, bf16[4,16,256]{2,1,0:T(8,128)(2,1)S(1)}, u32[]{:S(2)}, u32[]{:S(2)}) collective-permute-start(bf16[4,16,256]{2,1,0:T(8,128)(2,1)S(1)} %pad_maximum_fusion.1), channel_id=1, source_target_pairs={{0,2},{1,3},{2,0},{3,1},{4,6},{5,7},{6,4},{7,5},{8,10},{9,11},{10,... | collective-permute-start | bytes 98312 | tf_op jit(solution)/shard_map/ppermute | solution.py:173
  89.5 4.2 %collective-permute-done.3 = bf16[4,16,256]{2,1,0:T(8,128)(2,1)S(1)} collective-permute-done((bf16[4,16,256]{2,1,0:T(8,128)(2,1)S(1)}, bf16[4,16,256]{2,1,0:T(8,128)(2,1)S(1)}, u32[]{:S(2)}, u32[]{:S(2)}) %collective-permute-start.3) | collective-permute-done | bytes 32800 | tf_op jit(solution)/shard_map/ppermute | solution.py:173
  93.7 1.0 all-to-all-done.2
  94.7 0.9 reduce_sum.21
  95.6 7.6 %all-to-all-start.3 = ((bf16[8,64,256]{2,1,0:T(8,128)(2,1)}), bf16[8,64,256]{2,1,0:T(8,128)(2,1)S(1)}, u32[]{:S(2)}, u32[]{:S(2)}) async-start(bf16[8,64,256]{2,1,0:T(8,128)(2,1)} %bitcast.18), calls=%async_computation.3 | async-start | bytes 524288 | tf_op jit(solution)/shard_map/all_to_all | solution.py:145
  103.2 4.6 %collective-permute-start.4 = (bf16[4,16,256]{2,1,0:T(8,128)(2,1)S(1)}, bf16[4,16,256]{2,1,0:T(8,128)(2,1)S(1)}, u32[]{:S(2)}, u32[]{:S(2)}) collective-permute-start(bf16[4,16,256]{2,1,0:T(8,128)(2,1)S(1)} %pad_maximum_fusion.2), channel_id=1, source_target_pairs={{0,4},{1,5},{2,6},{3,7},{4,0},{5,1},{6,2},{7,3},{8,12},{9,13},{10,... | collective-permute-start | bytes 98312 | tf_op jit(solution)/shard_map/ppermute | solution.py:173
  107.9 2.7 %collective-permute-done.4 = bf16[4,16,256]{2,1,0:T(8,128)(2,1)S(1)} collective-permute-done((bf16[4,16,256]{2,1,0:T(8,128)(2,1)S(1)}, bf16[4,16,256]{2,1,0:T(8,128)(2,1)S(1)}, u32[]{:S(2)}, u32[]{:S(2)}) %collective-permute-start.4) | collective-permute-done | bytes 32800 | tf_op jit(solution)/shard_map/ppermute | solution.py:173
  110.6 13.6 %all-to-all-done.3 = bf16[8,64,256]{2,1,0:T(8,128)(2,1)S(1)} async-done(((bf16[8,64,256]{2,1,0:T(8,128)(2,1)}), bf16[8,64,256]{2,1,0:T(8,128)(2,1)S(1)}, u32[]{:S(2)}, u32[]{:S(2)}) %all-to-all-start.3) | async-done | bytes 262176 | tf_op jit(solution)/shard_map/all_to_all | solution.py:145
  124.3 0.0 copy-start.4
  124.3 0.7 convert_reduce_fusion
  125.0 0.0 copy-done.4
  (19 shorter events, 0.3 us)
Async XLA Ops:
  0.6 51.7 %copy-start.2 = (bf16[1,128,1024]{2,1,0:T(8,128)(2,1)S(1)}, bf16[1,128,1024]{2,1,0:T(8,128)(2,1)}, u32[]{:S(2)}) copy-start(bf16[1,128,1024]{2,1,0:T(8,128)(2,1)} %param.6) | copy-start | bytes 786436
  37.7 14.8 %copy-start.3 = (bf16[1,128,1024]{2,1,0:T(8,128)(2,1)S(1)}, bf16[1,128,1024]{2,1,0:T(8,128)(2,1)}, u32[]{:S(2)}) copy-start(bf16[1,128,1024]{2,1,0:T(8,128)(2,1)} %param.8) | copy-start | bytes 786436
  37.8 17.2 %copy-start = (bf16[1,128,256]{2,1,0:T(8,128)(2,1)S(1)}, bf16[1,128,256]{2,1,0:T(8,128)(2,1)}, u32[]{:S(2)}) copy-start(bf16[1,128,256]{2,1,0:T(8,128)(2,1)} %param.7) | copy-start | bytes 196612
  37.8 17.2 %copy-start.1 = (s32[64]{0:T(128)S(1)}, s32[64]{0:T(128)}, u32[]{:S(2)}) copy-start(s32[64]{0:T(128)} %lengths.1) | copy-start | bytes 772
  50.4 4.5 %collective-permute-start = (bf16[2048,256]{1,0:T(8,128)(2,1)S(1)}, bf16[2048,256]{1,0:T(8,128)(2,1)S(1)}, u32[]{:S(2)}, u32[]{:S(2)}) collective-permute-start(bf16[2048,256]{1,0:T(8,128)(2,1)S(1)} %bitcast.48), channel_id=1, source_target_pairs={{0,8},{8,0},{16,24},{24,16},{32,40},{40,32},{48,56},{56,48},{64,72... | collective-permute-start | bytes 3145736 | tf_op jit(solution)/shard_map/ppermute | solution.py:161
  71.2 4.5 %collective-permute-start.1 = (bf16[2048,256]{1,0:T(8,128)(2,1)S(1)}, bf16[2048,256]{1,0:T(8,128)(2,1)S(1)}, u32[]{:S(2)}, u32[]{:S(2)}) collective-permute-start(bf16[2048,256]{1,0:T(8,128)(2,1)S(1)} %get-tuple-element.29), channel_id=1, source_target_pairs={{0,8},{8,0},{16,24},{24,16},{32,40},{40,32},{48,56},{56,48},{64,72... | collective-permute-start | bytes 3145736 | tf_op jit(solution)/shard_map/ppermute | solution.py:167
  77.0 17.7 %all-to-all-start.2 = ((bf16[4,512,256]{2,1,0:T(8,128)(2,1)}), bf16[4,512,256]{2,1,0:T(8,128)(2,1)S(1)}, u32[]{:S(2)}, u32[]{:S(2)}) async-start(bf16[4,512,256]{2,1,0:T(8,128)(2,1)} %bitcast.9), calls=%async_computation.2 | async-start | bytes 2097152 | tf_op jit(solution)/shard_map/all_to_all | solution.py:145
  80.6 5.8 %collective-permute-start.2 = (bf16[4,16,256]{2,1,0:T(8,128)(2,1)S(1)}, bf16[4,16,256]{2,1,0:T(8,128)(2,1)S(1)}, u32[]{:S(2)}, u32[]{:S(2)}) collective-permute-start(bf16[4,16,256]{2,1,0:T(8,128)(2,1)S(1)} %pad_maximum_fusion), channel_id=1, source_target_pairs={{0,1},{1,0},{2,3},{3,2},{4,5},{5,4},{6,7},{7,6},{8,9},{9,8},{10,11... | collective-permute-start | bytes 98312 | tf_op jit(solution)/shard_map/ppermute | solution.py:173
  86.4 7.3 %collective-permute-start.3 = (bf16[4,16,256]{2,1,0:T(8,128)(2,1)S(1)}, bf16[4,16,256]{2,1,0:T(8,128)(2,1)S(1)}, u32[]{:S(2)}, u32[]{:S(2)}) collective-permute-start(bf16[4,16,256]{2,1,0:T(8,128)(2,1)S(1)} %pad_maximum_fusion.1), channel_id=1, source_target_pairs={{0,2},{1,3},{2,0},{3,1},{4,6},{5,7},{6,4},{7,5},{8,10},{9,11},{10,... | collective-permute-start | bytes 98312 | tf_op jit(solution)/shard_map/ppermute | solution.py:173
  95.6 28.5 %all-to-all-start.3 = ((bf16[8,64,256]{2,1,0:T(8,128)(2,1)}), bf16[8,64,256]{2,1,0:T(8,128)(2,1)S(1)}, u32[]{:S(2)}, u32[]{:S(2)}) async-start(bf16[8,64,256]{2,1,0:T(8,128)(2,1)} %bitcast.18), calls=%async_computation.3 | async-start | bytes 524288 | tf_op jit(solution)/shard_map/all_to_all | solution.py:145
  103.2 7.3 %collective-permute-start.4 = (bf16[4,16,256]{2,1,0:T(8,128)(2,1)S(1)}, bf16[4,16,256]{2,1,0:T(8,128)(2,1)S(1)}, u32[]{:S(2)}, u32[]{:S(2)}) collective-permute-start(bf16[4,16,256]{2,1,0:T(8,128)(2,1)S(1)} %pad_maximum_fusion.2), channel_id=1, source_target_pairs={{0,4},{1,5},{2,6},{3,7},{4,0},{5,1},{6,2},{7,3},{8,12},{9,13},{10,... | collective-permute-start | bytes 98312 | tf_op jit(solution)/shard_map/ppermute | solution.py:173
  124.3 0.7 copy-start.4

commit v5 on v4

--- a/solution.py
+++ b/solution.py
@@ -29,7 +29,7 @@
 
 def attention_kernel(
     lengths, order, head, qr, gr, own_ref, mine, other,
-    send_ref, keep_ref, d_own_ref, dq_ref, p_ref, d_own, *, width, group,
+    send_ref, keep_ref, d_own_ref, dq_ref, rest_ref, p_mine, p_other, d_own, *, width, group,
 ):
     rows = qr.shape[0]
     length = rows // group
@@ -41,7 +41,7 @@
         for at in range(0, count, CHUNK):
             here = pl.ds(at, CHUNK)
             k, v = kv.at[here, pl.ds(0, width)], kv.at[here, pl.ds(width, width)]
-            tiles.append((pl.ds(side * count + at, CHUNK), k, v, grads, here))
+            tiles.append(((p_other, p_mine)[side], here, k, v, grads))
 
     def eights(a):
         return a.reshape(a.shape[0] // 8, 8, rows)
@@ -52,7 +52,7 @@
     seen = lax.broadcasted_iota(jnp.int32, (length, rows), 0) <= slot
     s_own = jnp.where(seen, nt(own_k, qr[...]), NEG)
     m = jnp.max(eights(s_own), axis=0)
-    for at, k, v, grads, here in tiles:
+    for p_ref, at, k, v, grads in tiles:
         s = nt(k[...], qr[...])
         p_ref[at, :] = s
         m = jnp.maximum(m, jnp.max(eights(s), axis=0))
@@ -60,7 +60,7 @@
 
     p_own = jnp.exp2((s_own - top) * rate)
     l = jnp.sum(eights(p_own), axis=0)
-    for at, k, v, grads, here in tiles:
+    for p_ref, at, k, v, grads in tiles:
         p = jnp.exp2((p_ref[at, :] - top) * rate)
         p_ref[at, :] = p
         l = l + jnp.sum(eights(p), axis=0)
@@ -71,9 +71,12 @@
     w_own = p_own * factor
     w_own16 = w_own.astype(BF16)
     out = tn(own_v, w_own16)
-    for at, k, v, grads, here in tiles:
+    for p_ref, at, k, v, grads in tiles:
         w = (p_ref[at, :] * factor).astype(BF16)
-        grads[here, width:] = nn(w, gr[...]).astype(grads.dtype)
+        if grads is send_ref:
+            grads[at, width:] = nn(w, gr[...]).astype(grads.dtype)
+        else:
+            grads[at, :] = nn(w, gr[...])
         out = out + tn(v[...], w)
     delta = jnp.sum(gr[...].T.astype(F32) * out, axis=0, keepdims=True)
 
@@ -86,10 +89,25 @@
         d_own_ref[i] = d_own[pl.ds(at, slots), :]
     dq = tn(own_k, ds_own)
     factor = factor * scale
-    for at, k, v, grads, here in tiles:
+    for p_ref, at, k, v, grads in tiles[:len(tiles) // 2]:
         ds = (p_ref[at, :] * factor * (nt(v[...], gr[...]) - delta)).astype(BF16)
-        grads[here, :width] = nn(ds, qr[...]).astype(grads.dtype)
+        grads[at, :width] = nn(ds, qr[...]).astype(grads.dtype)
         dq = dq + tn(k[...], ds)
+    dq_ref[...] = dq
+    rest_ref[0:1, :] = factor
+    rest_ref[1:2, :] = delta
+    rest_ref[2:8, :] = jnp.zeros((6, rows), F32)
+
+
+def own_slopes_kernel(qr, gr, mine, p_mine, rest, dq_in, dk_ref, dq_ref, *, width, group):
+    length = qr.shape[0] // group
+    factor, delta = rest[0:1, :], rest[1:2, :]
+    dq = dq_in[...]
+    for start in range(0, mine.shape[0], CHUNK):
+        at = pl.ds(start, CHUNK)
+        ds = (p_mine[at, :] * factor * (nt(mine[at, width:], gr[...]) - delta)).astype(BF16)
+        dk_ref[at, :] = nn(ds, qr[...])
+        dq = dq + tn(mine[at, :width], ds)
     for h in range(group):
         part_h = dq[:, h * length:(h + 1) * length]
         dq_ref[:, h * width:(h + 1) * width] = part_h.T.astype(BF16)
@@ -104,26 +122,44 @@
     length = own.shape[0]
     group = rows // length
     count = mine.shape[0]
-    return pl.pallas_call(
+    params = pltpu.CompilerParams(vmem_limit_bytes=VMEM_LIMIT)
+    send, dv, d_own, dq, rest, p_mine = pl.pallas_call(
         functools.partial(attention_kernel, width=width, group=group),
         out_shape=[
             jax.ShapeDtypeStruct((count, 2 * width), BF16),
-            jax.ShapeDtypeStruct((count, 2 * width), F32),
+            jax.ShapeDtypeStruct((count, width), F32),
             jax.ShapeDtypeStruct((heads, length // heads, 2 * width), BF16),
-            jax.ShapeDtypeStruct((length, group * width), BF16),
+            jax.ShapeDtypeStruct((width, rows), F32),
+            jax.ShapeDtypeStruct((8, rows), F32),
+            jax.ShapeDtypeStruct((count, rows), F32),
         ],
         in_specs=[SM, SM, SM] + [VM] * 5,
-        out_specs=[VM] * 4,
+        out_specs=[VM] * 6,
         scratch_shapes=[
-            pltpu.VMEM((2 * count, rows), F32),
+            pltpu.VMEM((count, rows), F32),
             pltpu.VMEM((length, 2 * width), BF16),
         ],
-        compiler_params=pltpu.CompilerParams(vmem_limit_bytes=VMEM_LIMIT),
+        compiler_params=params,
         cost_estimate=pl.CostEstimate(
-            flops=24 * count * rows * width, bytes_accessed=1 << 23, transcendentals=0
+            flops=18 * count * rows * width, bytes_accessed=1 << 23, transcendentals=0
         ),
         name="attention",
     )(lengths, order, head, q, g, own, mine, other)
+    dk, d_query = pl.pallas_call(
+        functools.partial(own_slopes_kernel, width=width, group=group),
+        out_shape=[
+            jax.ShapeDtypeStruct((count, width), F32),
+            jax.ShapeDtypeStruct((length, group * width), BF16),
+        ],
+        in_specs=[VM] * 6,
+        out_specs=[VM] * 2,
+        compiler_params=params,
+        cost_estimate=pl.CostEstimate(
+            flops=60 * count * rows * width, bytes_accessed=1 << 23, transcendentals=0
+        ),
+        name="own_slopes",
+    )(q, g, mine, p_mine, rest, dq)
+    return send, jnp.concatenate([dk, dv], axis=1), d_own, d_query
 
 
 def per_device(query, resp_kv, grad_out, prefix_kv, lengths, order, *, layers, heads):

time: 125 us -> 125 us (level)
  waiting for transfers between devices: 28.8 us -> 26.7 us
    pallas_call x0 -> x1, Pallas kernels: none -> 3.76 us  [run_attention(): pl.pallas_call(functools.partial(own_slopes_kernel, width=width, group=gr...]
    pallas_call x1, Pallas kernels: 16.2 us -> 13.5 us  [run_attention(): pl.pallas_call(functools.partial(attention_kernel, width=width, group=gro...]
    ppermute x1, waiting for transfers between devices: 2.51 us -> 0.01 us  [per_device(): got = lax.ppermute(send, 'roll', to_core)]
  transfers between devices with their start and end apart: 7 -> 7, of which waited for: 7 -> 6; matrix products, arithmetic and copies ran while one was open for 0% -> 0% of each run, Pallas kernels for 0% -> 3%
where the time goes in v5:
time: 125 us; the launch traced here: 124 us
  blocking collectives  48.9 us (39%)
  waiting for transfers between devices  26.7 us (21%)
  starting transfers between devices  25.5 us (20%)
  Pallas kernels  17.3 us (14%)
  other arithmetic  2.98 us (2%)
  between operations  1.52 us (1%)
    all_to_all x2, blocking collectives, exchange(): lax.all_to_all(array, 'roll', split_axis=0, concat_axis=0, tiled=True, ax...  48.9 us
    all_to_all x2, waiting for transfers between devices, exchange(): lax.all_to_all(array, 'roll', split_axis=0, concat_axis=0, tiled=True, ax...  15 us
    pallas_call x1, Pallas kernels, run_attention(): pl.pallas_call(functools.partial(attention_kernel, width=width, group=gro...  13.5 us
    all_to_all x2, starting transfers between devices, exchange(): lax.all_to_all(array, 'roll', split_axis=0, concat_axis=0, tiled=True, ax...  11.1 us
    ppermute x3, starting transfers between devices, swap_heads(): lax.ppermute(jnp.stack([blocks[i] for i in sent]), 'head', [(i, i ^ bit)...  10.5 us
    ppermute x3, waiting for transfers between devices, swap_heads(): lax.ppermute(jnp.stack([blocks[i] for i in sent]), 'head', [(i, i ^ bit)...  9.97 us
    pallas_call x1, Pallas kernels, run_attention(): pl.pallas_call(functools.partial(own_slopes_kernel, width=width, group=gr...  3.76 us
  transfers between devices with their start and end apart: 7, of which 6 were waited for; matrix products, arithmetic and copies ran while one was open for 0% of the time, Pallas kernels for 3%

profile of v5, /device:TPU:24, one launch (start us, length us, event | category | flops | bytes accessed | tf_op | source)
XLA Modules:
  0.0 124.0 jit_solution(12382336983950792797)
XLA Ops:
  0.6 0.0 copy-start.2
  0.6 0.8 broadcast_in_dim.19
  1.5 36.3 %all_to_all.20 = bf16[8,64,256]{2,1,0:T(8,128)(2,1)S(1)} all-to-all(bf16[8,64,256]{2,1,0:T(8,128)(2,1)S(1)} %broadcast_in_dim.19), channel_id=1, replica_groups={{0,64,128,192,256,320,384,448},{8,72,136,200,264,328,392,456},{16,80,14..., dimensions={0} | all-to-all | bytes 524288 | tf_op jit(solution)/shard_map/all_to_all | solution.py:181
  37.7 0.1 broadcast_in_dim.21
  37.8 0.0 copy-start
  37.8 0.0 copy-start.1
  37.8 12.6 %all_to_all.21 = bf16[4,512,256]{2,1,0:T(8,128)(2,1)S(1)} all-to-all(bf16[4,512,256]{2,1,0:T(8,128)(2,1)S(1)} %broadcast_in_dim.21), channel_id=1, replica_groups={{0,16,32,48},{8,24,40,56},{64,80,96,112},{72,88,104,120},{128,144,160,1..., dimensions={0} | all-to-all | bytes 2097152 | tf_op jit(solution)/shard_map/all_to_all | solution.py:181
  50.4 1.9 %collective-permute-start = (bf16[2048,256]{1,0:T(8,128)(2,1)S(1)}, bf16[2048,256]{1,0:T(8,128)(2,1)S(1)}, u32[]{:S(2)}, u32[]{:S(2)}) collective-permute-start(bf16[2048,256]{1,0:T(8,128)(2,1)S(1)} %bitcast.48), channel_id=1, source_target_pairs={{0,8},{8,0},{16,24},{24,16},{32,40},{40,32},{48,56},{56,48},{64,72... | collective-permute-start | bytes 3145736 | tf_op jit(solution)/shard_map/ppermute | solution.py:197
  52.4 0.0 copy-done.2
  52.5 0.0 copy-done.3
  53.2 1.8 %collective-permute-done.other = bf16[2048,256]{1,0:T(8,128)(2,1)S(1)} collective-permute-done((bf16[2048,256]{1,0:T(8,128)(2,1)S(1)}, bf16[2048,256]{1,0:T(8,128)(2,1)S(1)}, u32[]{:S(2)}, u32[]{:S(2)}) %collective-permute-start) | collective-permute-done | bytes 1048608 | tf_op jit(solution)/shard_map/ppermute | solution.py:197
  55.0 0.0 copy-done
  55.0 0.0 copy-done.1
  55.0 13.5 %attention.1 = (bf16[2048,256]{1,0:T(8,128)(2,1)S(1)}, f32[2048,128]{1,0:T(8,128)S(1)}, bf16[8,16,256]{2,1,0:T(8,128)(2,1)S(1)}, f32[128,1024]{1,0:T(8,128)S(1)}...) custom-call(s32[64]{0:T(128)S(1)} %copy-done.1, s32[1]{0:T(128)S(6)} %copy.22.order, s32[1]{0:T(128)} %bitcast.6.head, ...), custom_call_target="tpu_custom_call" | custom-call | flops 4831838208 | bytes 8388608 | tf_op jit(solution)/shard_map/attention/pallas_call | solution.py:126
  68.5 2.0 %collective-permute-start.1 = (bf16[2048,256]{1,0:T(8,128)(2,1)S(1)}, bf16[2048,256]{1,0:T(8,128)(2,1)S(1)}, u32[]{:S(2)}, u32[]{:S(2)}) collective-permute-start(bf16[2048,256]{1,0:T(8,128)(2,1)S(1)} %get-tuple-element.37), channel_id=1, source_target_pairs={{0,8},{8,0},{16,24},{24,16},{32,40},{40,32},{48,56},{56,48},{64,72... | collective-permute-start | bytes 3145736 | tf_op jit(solution)/shard_map/ppermute | solution.py:203
  70.6 3.8 %own_slopes.1 = (f32[2048,128]{1,0:T(8,128)S(1)}, bf16[128,1024]{1,0:T(8,128)(2,1)}) custom-call(bf16[1024,128]{1,0:T(8,128)(2,1)S(1)} %bitcast.52, bf16[1024,128]{1,0:T(8,128)(2,1)S(1)} %bitcast.54, bf16[2048,256]{1,0:T(8,128)(2,1)S(1)} %bitcast.50, f32[2048,1024]{1,0:T(8,128)S(1)} %get-tuple-element.31.p_mine, f32[8,1024]{1,0:T(8,128)S(1)} %get-tuple-element.32.rest, ...), custom_call_target="tpu_custom_call" | custom-call | flops 16106127360 | bytes 8388608 | tf_op jit(solution)/shard_map/own_slopes/pallas_call | solution.py:148
  74.4 0.0 collective-permute-done.1
  74.4 1.3 %fusion = bf16[2048,256]{1,0:T(8,128)(2,1)} fusion(f32[2048,128]{1,0:T(8,128)S(1)} %get-tuple-element.36, f32[2048,128]{1,0:T(8,128)S(1)} %get-tuple-element.35, bf16[2048,256]{1,0:T(8,128)(2,1)S(1)} %collective-permute-done.1), kind=kLoop, calls=%fused_computation.1 | loop fusion | flops 2097152 | bytes 4194304 | tf_op jit(solution)/shard_map/convert_element_type | solution.py:204
  75.7 3.5 %all-to-all-start.2 = ((bf16[4,512,256]{2,1,0:T(8,128)(2,1)}), bf16[4,512,256]{2,1,0:T(8,128)(2,1)S(1)}, u32[]{:S(2)}, u32[]{:S(2)}) async-start(bf16[4,512,256]{2,1,0:T(8,128)(2,1)} %bitcast.11), calls=%async_computation.2 | async-start | bytes 2097152 | tf_op jit(solution)/shard_map/all_to_all | solution.py:181
  79.2 2.7 %collective-permute-start.2 = (bf16[4,16,256]{2,1,0:T(8,128)(2,1)S(1)}, bf16[4,16,256]{2,1,0:T(8,128)(2,1)S(1)}, u32[]{:S(2)}, u32[]{:S(2)}) collective-permute-start(bf16[4,16,256]{2,1,0:T(8,128)(2,1)S(1)} %pad_maximum_fusion), channel_id=1, source_target_pairs={{0,1},{1,0},{2,3},{3,2},{4,5},{5,4},{6,7},{7,6},{8,9},{9,8},{10,11... | collective-permute-start | bytes 98312 | tf_op jit(solution)/shard_map/ppermute | solution.py:209
  81.9 3.1 %collective-permute-done.2 = bf16[4,16,256]{2,1,0:T(8,128)(2,1)S(1)} collective-permute-done((bf16[4,16,256]{2,1,0:T(8,128)(2,1)S(1)}, bf16[4,16,256]{2,1,0:T(8,128)(2,1)S(1)}, u32[]{:S(2)}, u32[]{:S(2)}) %collective-permute-start.2) | collective-permute-done | bytes 32800 | tf_op jit(solution)/shard_map/ppermute | solution.py:209
  85.1 3.1 %collective-permute-start.3 = (bf16[4,16,256]{2,1,0:T(8,128)(2,1)S(1)}, bf16[4,16,256]{2,1,0:T(8,128)(2,1)S(1)}, u32[]{:S(2)}, u32[]{:S(2)}) collective-permute-start(bf16[4,16,256]{2,1,0:T(8,128)(2,1)S(1)} %pad_maximum_fusion.1), channel_id=1, source_target_pairs={{0,2},{1,3},{2,0},{3,1},{4,6},{5,7},{6,4},{7,5},{8,10},{9,11},{10,... | collective-permute-start | bytes 98312 | tf_op jit(solution)/shard_map/ppermute | solution.py:209
  88.2 4.2 %collective-permute-done.3 = bf16[4,16,256]{2,1,0:T(8,128)(2,1)S(1)} collective-permute-done((bf16[4,16,256]{2,1,0:T(8,128)(2,1)S(1)}, bf16[4,16,256]{2,1,0:T(8,128)(2,1)S(1)}, u32[]{:S(2)}, u32[]{:S(2)}) %collective-permute-start.3) | collective-permute-done | bytes 32800 | tf_op jit(solution)/shard_map/ppermute | solution.py:209
  92.4 1.2 all-to-all-done.2
  93.6 0.9 reduce_sum.21
  94.5 7.6 %all-to-all-start.3 = ((bf16[8,64,256]{2,1,0:T(8,128)(2,1)}), bf16[8,64,256]{2,1,0:T(8,128)(2,1)S(1)}, u32[]{:S(2)}, u32[]{:S(2)}) async-start(bf16[8,64,256]{2,1,0:T(8,128)(2,1)} %bitcast.20), calls=%async_computation.3 | async-start | bytes 524288 | tf_op jit(solution)/shard_map/all_to_all | solution.py:181
  102.1 4.6 %collective-permute-start.4 = (bf16[4,16,256]{2,1,0:T(8,128)(2,1)S(1)}, bf16[4,16,256]{2,1,0:T(8,128)(2,1)S(1)}, u32[]{:S(2)}, u32[]{:S(2)}) collective-permute-start(bf16[4,16,256]{2,1,0:T(8,128)(2,1)S(1)} %pad_maximum_fusion.2), channel_id=1, source_target_pairs={{0,4},{1,5},{2,6},{3,7},{4,0},{5,1},{6,2},{7,3},{8,12},{9,13},{10,... | collective-permute-start | bytes 98312 | tf_op jit(solution)/shard_map/ppermute | solution.py:209
  106.8 2.7 %collective-permute-done.4 = bf16[4,16,256]{2,1,0:T(8,128)(2,1)S(1)} collective-permute-done((bf16[4,16,256]{2,1,0:T(8,128)(2,1)S(1)}, bf16[4,16,256]{2,1,0:T(8,128)(2,1)S(1)}, u32[]{:S(2)}, u32[]{:S(2)}) %collective-permute-start.4) | collective-permute-done | bytes 32800 | tf_op jit(solution)/shard_map/ppermute | solution.py:209
  109.4 13.7 %all-to-all-done.3 = bf16[8,64,256]{2,1,0:T(8,128)(2,1)S(1)} async-done(((bf16[8,64,256]{2,1,0:T(8,128)(2,1)}), bf16[8,64,256]{2,1,0:T(8,128)(2,1)S(1)}, u32[]{:S(2)}, u32[]{:S(2)}) %all-to-all-start.3) | async-done | bytes 262176 | tf_op jit(solution)/shard_map/all_to_all | solution.py:181
  123.3 0.0 copy-start.4
  123.3 0.7 convert_reduce_fusion
  124.0 0.0 copy-done.4
  (20 shorter events, 0.3 us)
Async XLA Ops:
  0.6 51.7 %copy-start.2 = (bf16[1,128,1024]{2,1,0:T(8,128)(2,1)S(1)}, bf16[1,128,1024]{2,1,0:T(8,128)(2,1)}, u32[]{:S(2)}) copy-start(bf16[1,128,1024]{2,1,0:T(8,128)(2,1)} %param.6) | copy-start | bytes 786436
  37.7 14.8 %copy-start.3 = (bf16[1,128,1024]{2,1,0:T(8,128)(2,1)S(1)}, bf16[1,128,1024]{2,1,0:T(8,128)(2,1)}, u32[]{:S(2)}) copy-start(bf16[1,128,1024]{2,1,0:T(8,128)(2,1)} %param.8) | copy-start | bytes 786436
  37.8 17.2 %copy-start = (bf16[1,128,256]{2,1,0:T(8,128)(2,1)S(1)}, bf16[1,128,256]{2,1,0:T(8,128)(2,1)}, u32[]{:S(2)}) copy-start(bf16[1,128,256]{2,1,0:T(8,128)(2,1)} %param.7) | copy-start | bytes 196612
  37.8 17.2 %copy-start.1 = (s32[64]{0:T(128)S(1)}, s32[64]{0:T(128)}, u32[]{:S(2)}) copy-start(s32[64]{0:T(128)} %lengths.1) | copy-start | bytes 772
  50.4 4.5 %collective-permute-start = (bf16[2048,256]{1,0:T(8,128)(2,1)S(1)}, bf16[2048,256]{1,0:T(8,128)(2,1)S(1)}, u32[]{:S(2)}, u32[]{:S(2)}) collective-permute-start(bf16[2048,256]{1,0:T(8,128)(2,1)S(1)} %bitcast.48), channel_id=1, source_target_pairs={{0,8},{8,0},{16,24},{24,16},{32,40},{40,32},{48,56},{56,48},{64,72... | collective-permute-start | bytes 3145736 | tf_op jit(solution)/shard_map/ppermute | solution.py:197
  68.5 5.8 %collective-permute-start.1 = (bf16[2048,256]{1,0:T(8,128)(2,1)S(1)}, bf16[2048,256]{1,0:T(8,128)(2,1)S(1)}, u32[]{:S(2)}, u32[]{:S(2)}) collective-permute-start(bf16[2048,256]{1,0:T(8,128)(2,1)S(1)} %get-tuple-element.37), channel_id=1, source_target_pairs={{0,8},{8,0},{16,24},{24,16},{32,40},{40,32},{48,56},{56,48},{64,72... | collective-permute-start | bytes 3145736 | tf_op jit(solution)/shard_map/ppermute | solution.py:203
  75.7 17.9 %all-to-all-start.2 = ((bf16[4,512,256]{2,1,0:T(8,128)(2,1)}), bf16[4,512,256]{2,1,0:T(8,128)(2,1)S(1)}, u32[]{:S(2)}, u32[]{:S(2)}) async-start(bf16[4,512,256]{2,1,0:T(8,128)(2,1)} %bitcast.11), calls=%async_computation.2 | async-start | bytes 2097152 | tf_op jit(solution)/shard_map/all_to_all | solution.py:181
  79.2 5.8 %collective-permute-start.2 = (bf16[4,16,256]{2,1,0:T(8,128)(2,1)S(1)}, bf16[4,16,256]{2,1,0:T(8,128)(2,1)S(1)}, u32[]{:S(2)}, u32[]{:S(2)}) collective-permute-start(bf16[4,16,256]{2,1,0:T(8,128)(2,1)S(1)} %pad_maximum_fusion), channel_id=1, source_target_pairs={{0,1},{1,0},{2,3},{3,2},{4,5},{5,4},{6,7},{7,6},{8,9},{9,8},{10,11... | collective-permute-start | bytes 98312 | tf_op jit(solution)/shard_map/ppermute | solution.py:209
  85.1 7.3 %collective-permute-start.3 = (bf16[4,16,256]{2,1,0:T(8,128)(2,1)S(1)}, bf16[4,16,256]{2,1,0:T(8,128)(2,1)S(1)}, u32[]{:S(2)}, u32[]{:S(2)}) collective-permute-start(bf16[4,16,256]{2,1,0:T(8,128)(2,1)S(1)} %pad_maximum_fusion.1), channel_id=1, source_target_pairs={{0,2},{1,3},{2,0},{3,1},{4,6},{5,7},{6,4},{7,5},{8,10},{9,11},{10,... | collective-permute-start | bytes 98312 | tf_op jit(solution)/shard_map/ppermute | solution.py:209
  94.5 28.7 %all-to-all-start.3 = ((bf16[8,64,256]{2,1,0:T(8,128)(2,1)}), bf16[8,64,256]{2,1,0:T(8,128)(2,1)S(1)}, u32[]{:S(2)}, u32[]{:S(2)}) async-start(bf16[8,64,256]{2,1,0:T(8,128)(2,1)} %bitcast.20), calls=%async_computation.3 | async-start | bytes 524288 | tf_op jit(solution)/shard_map/all_to_all | solution.py:181
  102.1 7.3 %collective-permute-start.4 = (bf16[4,16,256]{2,1,0:T(8,128)(2,1)S(1)}, bf16[4,16,256]{2,1,0:T(8,128)(2,1)S(1)}, u32[]{:S(2)}, u32[]{:S(2)}) collective-permute-start(bf16[4,16,256]{2,1,0:T(8,128)(2,1)S(1)} %pad_maximum_fusion.2), channel_id=1, source_target_pairs={{0,4},{1,5},{2,6},{3,7},{4,0},{5,1},{6,2},{7,3},{8,12},{9,13},{10,... | collective-permute-start | bytes 98312 | tf_op jit(solution)/shard_map/ppermute | solution.py:209
  123.3 0.7 copy-start.4
